TPU v7x, 128 devices: a whole 4x4x4 slice. The times are simulated.
128 devices in a mesh: grp: 8 (over x, core), sib: 16 (over y, z).
Axes of the slice: x: 4, y: 4, z: 4, core: 2. Of those that a mesh axis runs over, the one named last changes fastest.
Arguments:
- density: bfloat16 [1024, 512, 512], P(('grp', 'sib')), may hold values from -9 to 9
- kernel: bfloat16 [512, 256], replicated, may hold values from -0.25 to 0.25
- transfer: float32 [4, 256, 256], replicated, may hold values from -1 to 2, as said below
- target_device: int32 [1024, 16], replicated, may hold values from 0 to 127, all different within a row; in each aligned block of 8 rows (0 to 7, 8 to 15, ...) at most 2 rows name the same one
- target_slot: int32 [1024, 16], replicated, may hold values from 0 to 7
- cycle_rows: int32 [1024, 32], replicated, may hold values from 0 to 511, as said below
Outputs:
- leaf_factor: float32 [1024, 256, 256], P(('grp', 'sib'))
- tree_factor: float32 [128, 256, 256], P(('grp', 'sib'))
Inputs may be any that keep to these rules, and one draw needn't show every extreme that they name: `target_device`: each row names distinct devices; the 8 rows of one device name each device at most 2 times, and some device exactly 2 times. Each level's transfer matrix is invertible. `cycle_rows`: the cycle of each target cluster lies within one of the four blocks of 128 consecutive longitudes.
All inputs are finite; a program needn't handle non-finite values.
Results may differ from a plain program's by a relative error of at most 0.0024.
Values may be sent and summed in bfloat16 or wider, within the bound.
A program may use at most 64 MiB of HBM per device.

v0:
```python
import jax
import jax.numpy as jnp
from jax import lax
from jax.sharding import PartitionSpec as P


def from_partner(value, axis, bit):
    mask = 2**bit
    pairs = [(source, source ^ mask) for source in range(lax.axis_size(axis))]
    return lax.ppermute(value, axis, pairs)


def congruent(matrix, factor):
    inner = jnp.matmul(factor.T, matrix, precision=lax.Precision.HIGHEST)
    return jnp.matmul(inner, factor, precision=lax.Precision.HIGHEST)


def rescale(matrix):
    width = matrix.shape[-1]
    traces = jnp.trace(matrix, axis1=-2, axis2=-1)
    return width * matrix / traces[..., None, None]


def group_pair(matrix, bit_index):
    return matrix + from_partner(matrix, "grp", bit_index)


def local(density, kernel, transfer, target_device, target_slot, cycle_rows):
    n_grp = lax.axis_size("grp")
    n_sib = lax.axis_size("sib")
    devices = n_grp * n_sib
    own_index = lax.axis_index("grp") * n_sib + lax.axis_index("sib")
    leaf_dev = density.shape[0]
    n_list = target_device.shape[1]
    cycle_len = cycle_rows.shape[1]
    rank = kernel.shape[1]
    capacity = max(2, 2 * leaf_dev * n_list // devices)
    slots = devices * capacity
    entries = leaf_dev * n_list
    correlated = jnp.einsum(
        "slc,cr->slr", density, kernel, preferred_element_type=jnp.float32
    ).astype(jnp.bfloat16)
    own_dest = lax.dynamic_slice_in_dim(target_device, own_index * leaf_dev, leaf_dev, 0).reshape(
        entries
    )
    own_local = lax.dynamic_slice_in_dim(target_slot, own_index * leaf_dev, leaf_dev, 0).reshape(
        entries
    )
    device_iota = jnp.arange(devices, dtype=jnp.int32)
    dest_hits = (own_dest[:, None] == device_iota[None, :]).astype(jnp.int32)
    ahead = jnp.sum((jnp.cumsum(dest_hits, axis=0) - dest_hits) * dest_hits, axis=1)
    slot_of = own_dest * capacity + ahead
    entry_of = (
        jnp.full((slots,), -1, jnp.int32).at[slot_of].set(jnp.arange(entries, dtype=jnp.int32))
    )
    filled = entry_of >= 0
    entry_safe = jnp.maximum(entry_of, 0)
    source_leaf = entry_safe // n_list
    target_global = own_dest[entry_safe] * leaf_dev + own_local[entry_safe]
    cycle_pick = cycle_rows[target_global]
    outgoing = correlated[source_leaf[:, None], cycle_pick]
    outgoing = jnp.where(filled[:, None, None], outgoing, jnp.zeros_like(outgoing))
    flat_send = outgoing.reshape(devices, capacity, cycle_len, rank)
    arrived = lax.all_to_all(flat_send, ("grp", "sib"), split_axis=0, concat_axis=0, tiled=True)
    arrived = arrived.reshape(slots, cycle_len, rank)
    block_dest = target_device.reshape(devices, entries)
    block_local = target_slot.reshape(devices, entries)
    incoming = (block_dest == own_index).astype(jnp.int32)
    before = jnp.cumsum(incoming, axis=1) - incoming
    slot_iota = jnp.arange(capacity, dtype=jnp.int32)
    placed = (incoming[:, :, None] * (before[:, :, None] == slot_iota[None, None, :])).astype(
        jnp.float32
    )
    leaf_iota = jnp.arange(leaf_dev, dtype=jnp.int32)
    matches = (block_local[:, :, None] == leaf_iota[None, None, :]).astype(jnp.float32)
    weights = jnp.einsum("dec,dej->dcj", placed, matches, precision=lax.Precision.HIGHEST).reshape(
        slots, leaf_dev
    )
    group_size = 16
    groups = slots // group_size
    slot_blocks = arrived.reshape(groups, group_size, cycle_len, rank)
    weight_blocks = weights.reshape(groups, group_size, leaf_dev)

    def add_group(running, element):
        block_rows, block_weights = element
        slot_grams = jnp.einsum(
            "srk,srl->skl", block_rows, block_rows, preferred_element_type=jnp.float32
        )
        update = jnp.einsum(
            "sj,skl->jkl", block_weights, slot_grams, precision=lax.Precision.HIGHEST
        )
        return (running + update, None)

    running, _ = lax.scan(
        add_group, jnp.zeros((leaf_dev, rank, rank), jnp.float32), (slot_blocks, weight_blocks)
    )
    identity = jnp.eye(rank, dtype=jnp.float32)
    gram = identity[None] + running / cycle_len
    leaf_factor = jnp.linalg.cholesky(gram)
    first_level = congruent(
        rescale(gram).reshape(leaf_dev // 4, 4, rank, rank).sum(axis=1), transfer[0]
    )
    current = rescale(first_level).sum(axis=0)
    level_bits = ((0,), (1, 2), (3, 4))
    sib_bits = n_sib.bit_length() - 1
    for level_index, bit_list in enumerate(level_bits):
        if level_index > 0:
            current = rescale(current)
        for bit_index in bit_list:
            if bit_index < sib_bits:
                current = current + from_partner(current, "sib", bit_index)
            else:
                current = group_pair(current, bit_index - sib_bits)
        current = congruent(current, transfer[level_index + 1])
    root_factor = jnp.linalg.cholesky(current)
    return (leaf_factor, root_factor[None])


def solution(mesh):
    return jax.shard_map(
        local,
        mesh=mesh,
        in_specs=(P(("grp", "sib"), None, None), P(), P(), P(), P(), P()),
        out_specs=(P(("grp", "sib"), None, None), P(("grp", "sib"), None, None)),
        check_vma=False,
    )
```

profile of v0, /device:TPU:1, one launch (start us, length us, event | category | flops | bytes accessed | tf_op | source)
XLA Modules:
  0.0 689.9 jit_solution(6395945456764151019)
XLA Ops:
  3.3 1.9 gather_fusion
  5.3 1.9 gather_fusion.1
  8.5 3.4 convolution_convert_fusion
  12.0 80.9 %gather_fusion.3 = bf16[8192,256]{1,0:T(8,128)(2,1)} fusion(bf16[8,512,256]{2,1,0:T(8,128)(2,1)S(1)} %convolution_convert_fusion, s32[8192]{0:T(1024)S(1)} %reshape.186), kind=kCustom, calls=%fused_computation.3 | custom fusion | bytes 8454144 | tf_op jit(solution)/shard_map/gather | solution.py:61
  92.9 3.8 broadcast_select_fusion
  96.6 12.4 %all-to-all-start = ((bf16[128,2,32,256]{3,2,1,0:T(8,128)(2,1)}), bf16[128,2,32,256]{3,2,1,0:T(8,128)(2,1)}, u32[]{:S(2)}, u32[]{:S(2)}) async-start(bf16[128,2,32,256]{3,2,1,0:T(8,128)(2,1)} %broadcast_select_fusion), calls=%async_computation | async-start | bytes 8388608 | tf_op jit(solution)/shard_map/all_to_all | solution.py:64
  112.2 48.8 %all-to-all-done = bf16[128,2,32,256]{3,2,1,0:T(8,128)(2,1)} async-done(((bf16[128,2,32,256]{3,2,1,0:T(8,128)(2,1)}), bf16[128,2,32,256]{3,2,1,0:T(8,128)(2,1)}, u32[]{:S(2)}, u32[]{:S(2)}) %all-to-all-start) | async-done | bytes 4194336 | tf_op jit(solution)/shard_map/all_to_all | solution.py:64
  161.0 172.6 %while.11 = (s32[]{:T(128)}, f32[8,256,256]{2,0,1:T(8,128)S(1)}, f32[16,16,8]{1,2,0:T(8,128)S(1)}, bf16[16,16,32,256]{3,2,1,0:T(8,128)(2,1)}, s32[]{:T(128)}, /*index=5*/s32[]{:T(128)}) while((s32[]{:T(128)}, f32[8,256,256]{2,0,1:T(8,128)S(1)}, f32[16,16,8]{1,2,0:T(8,128)S(1)}, bf16[16,16,32,256]{3,2,1,0:T(8,128)(2,1)}, s32[]{:T(128)}, ...), condition=%wide.region_5.6_spmd.clone, body=%wide.region_4.5_spmd.clone.sunk | while | flops 168820736 | bytes 12849747 | solution.py:94
  161.0 3.7 fusion.84
  164.8 7.0 %select_add_fusion.2 = f32[8,256,256]{2,0,1:T(8,128)S(1)} fusion(f32[8,256,256]{2,0,1:T(8,128)S(1)} %get-tuple-element.130, f32[16,256,256]{2,1,0:T(8,128)} %fusion.84, pred[]{:T(512)S(6)} %compare.40, f32[16,16,8]{1,2,0:T(8,128)S(1)} %get-tuple-element.137, s32[]{:T(128)} %get-tuple-element.129), kind=kOutput, calls=%fused_computation.7.clone.1 | convolution fusion | flops 101711872 | bytes 8392709 | tf_op jit(solution)/shard_map/while/body/eval_jaxpr/sj,skl->jkl/dot_general | solution.py:89
  171.8 3.8 fusion.84
  175.5 7.0 %select_add_fusion.2 = f32[8,256,256]{2,0,1:T(8,128)S(1)} fusion(f32[8,256,256]{2,0,1:T(8,128)S(1)} %get-tuple-element.130, f32[16,256,256]{2,1,0:T(8,128)} %fusion.84, pred[]{:T(512)S(6)} %compare.40, f32[16,16,8]{1,2,0:T(8,128)S(1)} %get-tuple-element.137, s32[]{:T(128)} %get-tuple-element.129), kind=kOutput, calls=%fused_computation.7.clone.1 | convolution fusion | flops 101711872 | bytes 8392709 | tf_op jit(solution)/shard_map/while/body/eval_jaxpr/sj,skl->jkl/dot_general | solution.py:89
  182.6 3.8 fusion.84
  186.3 7.0 %select_add_fusion.2 = f32[8,256,256]{2,0,1:T(8,128)S(1)} fusion(f32[8,256,256]{2,0,1:T(8,128)S(1)} %get-tuple-element.130, f32[16,256,256]{2,1,0:T(8,128)} %fusion.84, pred[]{:T(512)S(6)} %compare.40, f32[16,16,8]{1,2,0:T(8,128)S(1)} %get-tuple-element.137, s32[]{:T(128)} %get-tuple-element.129), kind=kOutput, calls=%fused_computation.7.clone.1 | convolution fusion | flops 101711872 | bytes 8392709 | tf_op jit(solution)/shard_map/while/body/eval_jaxpr/sj,skl->jkl/dot_general | solution.py:89
  193.4 3.8 fusion.84
  197.1 7.0 %select_add_fusion.2 = f32[8,256,256]{2,0,1:T(8,128)S(1)} fusion(f32[8,256,256]{2,0,1:T(8,128)S(1)} %get-tuple-element.130, f32[16,256,256]{2,1,0:T(8,128)} %fusion.84, pred[]{:T(512)S(6)} %compare.40, f32[16,16,8]{1,2,0:T(8,128)S(1)} %get-tuple-element.137, s32[]{:T(128)} %get-tuple-element.129), kind=kOutput, calls=%fused_computation.7.clone.1 | convolution fusion | flops 101711872 | bytes 8392709 | tf_op jit(solution)/shard_map/while/body/eval_jaxpr/sj,skl->jkl/dot_general | solution.py:89
  204.1 3.8 fusion.84
  207.9 7.0 %select_add_fusion.2 = f32[8,256,256]{2,0,1:T(8,128)S(1)} fusion(f32[8,256,256]{2,0,1:T(8,128)S(1)} %get-tuple-element.130, f32[16,256,256]{2,1,0:T(8,128)} %fusion.84, pred[]{:T(512)S(6)} %compare.40, f32[16,16,8]{1,2,0:T(8,128)S(1)} %get-tuple-element.137, s32[]{:T(128)} %get-tuple-element.129), kind=kOutput, calls=%fused_computation.7.clone.1 | convolution fusion | flops 101711872 | bytes 8392709 | tf_op jit(solution)/shard_map/while/body/eval_jaxpr/sj,skl->jkl/dot_general | solution.py:89
  214.9 3.8 fusion.84
  218.7 7.0 %select_add_fusion.2 = f32[8,256,256]{2,0,1:T(8,128)S(1)} fusion(f32[8,256,256]{2,0,1:T(8,128)S(1)} %get-tuple-element.130, f32[16,256,256]{2,1,0:T(8,128)} %fusion.84, pred[]{:T(512)S(6)} %compare.40, f32[16,16,8]{1,2,0:T(8,128)S(1)} %get-tuple-element.137, s32[]{:T(128)} %get-tuple-element.129), kind=kOutput, calls=%fused_computation.7.clone.1 | convolution fusion | flops 101711872 | bytes 8392709 | tf_op jit(solution)/shard_map/while/body/eval_jaxpr/sj,skl->jkl/dot_general | solution.py:89
  225.7 3.8 fusion.84
  229.5 7.0 %select_add_fusion.2 = f32[8,256,256]{2,0,1:T(8,128)S(1)} fusion(f32[8,256,256]{2,0,1:T(8,128)S(1)} %get-tuple-element.130, f32[16,256,256]{2,1,0:T(8,128)} %fusion.84, pred[]{:T(512)S(6)} %compare.40, f32[16,16,8]{1,2,0:T(8,128)S(1)} %get-tuple-element.137, s32[]{:T(128)} %get-tuple-element.129), kind=kOutput, calls=%fused_computation.7.clone.1 | convolution fusion | flops 101711872 | bytes 8392709 | tf_op jit(solution)/shard_map/while/body/eval_jaxpr/sj,skl->jkl/dot_general | solution.py:89
  236.5 3.8 fusion.84
  240.3 7.0 %select_add_fusion.2 = f32[8,256,256]{2,0,1:T(8,128)S(1)} fusion(f32[8,256,256]{2,0,1:T(8,128)S(1)} %get-tuple-element.130, f32[16,256,256]{2,1,0:T(8,128)} %fusion.84, pred[]{:T(512)S(6)} %compare.40, f32[16,16,8]{1,2,0:T(8,128)S(1)} %get-tuple-element.137, s32[]{:T(128)} %get-tuple-element.129), kind=kOutput, calls=%fused_computation.7.clone.1 | convolution fusion | flops 101711872 | bytes 8392709 | tf_op jit(solution)/shard_map/while/body/eval_jaxpr/sj,skl->jkl/dot_general | solution.py:89
  247.3 3.8 fusion.84
  251.0 7.0 %select_add_fusion.2 = f32[8,256,256]{2,0,1:T(8,128)S(1)} fusion(f32[8,256,256]{2,0,1:T(8,128)S(1)} %get-tuple-element.130, f32[16,256,256]{2,1,0:T(8,128)} %fusion.84, pred[]{:T(512)S(6)} %compare.40, f32[16,16,8]{1,2,0:T(8,128)S(1)} %get-tuple-element.137, s32[]{:T(128)} %get-tuple-element.129), kind=kOutput, calls=%fused_computation.7.clone.1 | convolution fusion | flops 101711872 | bytes 8392709 | tf_op jit(solution)/shard_map/while/body/eval_jaxpr/sj,skl->jkl/dot_general | solution.py:89
  258.1 3.8 fusion.84
  261.8 7.0 %select_add_fusion.2 = f32[8,256,256]{2,0,1:T(8,128)S(1)} fusion(f32[8,256,256]{2,0,1:T(8,128)S(1)} %get-tuple-element.130, f32[16,256,256]{2,1,0:T(8,128)} %fusion.84, pred[]{:T(512)S(6)} %compare.40, f32[16,16,8]{1,2,0:T(8,128)S(1)} %get-tuple-element.137, s32[]{:T(128)} %get-tuple-element.129), kind=kOutput, calls=%fused_computation.7.clone.1 | convolution fusion | flops 101711872 | bytes 8392709 | tf_op jit(solution)/shard_map/while/body/eval_jaxpr/sj,skl->jkl/dot_general | solution.py:89
  268.9 3.8 fusion.84
  272.6 7.0 %select_add_fusion.2 = f32[8,256,256]{2,0,1:T(8,128)S(1)} fusion(f32[8,256,256]{2,0,1:T(8,128)S(1)} %get-tuple-element.130, f32[16,256,256]{2,1,0:T(8,128)} %fusion.84, pred[]{:T(512)S(6)} %compare.40, f32[16,16,8]{1,2,0:T(8,128)S(1)} %get-tuple-element.137, s32[]{:T(128)} %get-tuple-element.129), kind=kOutput, calls=%fused_computation.7.clone.1 | convolution fusion | flops 101711872 | bytes 8392709 | tf_op jit(solution)/shard_map/while/body/eval_jaxpr/sj,skl->jkl/dot_general | solution.py:89
  279.7 3.8 fusion.84
  283.4 7.0 %select_add_fusion.2 = f32[8,256,256]{2,0,1:T(8,128)S(1)} fusion(f32[8,256,256]{2,0,1:T(8,128)S(1)} %get-tuple-element.130, f32[16,256,256]{2,1,0:T(8,128)} %fusion.84, pred[]{:T(512)S(6)} %compare.40, f32[16,16,8]{1,2,0:T(8,128)S(1)} %get-tuple-element.137, s32[]{:T(128)} %get-tuple-element.129), kind=kOutput, calls=%fused_computation.7.clone.1 | convolution fusion | flops 101711872 | bytes 8392709 | tf_op jit(solution)/shard_map/while/body/eval_jaxpr/sj,skl->jkl/dot_general | solution.py:89
  290.4 3.8 fusion.84
  294.2 7.0 %select_add_fusion.2 = f32[8,256,256]{2,0,1:T(8,128)S(1)} fusion(f32[8,256,256]{2,0,1:T(8,128)S(1)} %get-tuple-element.130, f32[16,256,256]{2,1,0:T(8,128)} %fusion.84, pred[]{:T(512)S(6)} %compare.40, f32[16,16,8]{1,2,0:T(8,128)S(1)} %get-tuple-element.137, s32[]{:T(128)} %get-tuple-element.129), kind=kOutput, calls=%fused_computation.7.clone.1 | convolution fusion | flops 101711872 | bytes 8392709 | tf_op jit(solution)/shard_map/while/body/eval_jaxpr/sj,skl->jkl/dot_general | solution.py:89
  301.2 3.8 fusion.84
  305.0 7.0 %select_add_fusion.2 = f32[8,256,256]{2,0,1:T(8,128)S(1)} fusion(f32[8,256,256]{2,0,1:T(8,128)S(1)} %get-tuple-element.130, f32[16,256,256]{2,1,0:T(8,128)} %fusion.84, pred[]{:T(512)S(6)} %compare.40, f32[16,16,8]{1,2,0:T(8,128)S(1)} %get-tuple-element.137, s32[]{:T(128)} %get-tuple-element.129), kind=kOutput, calls=%fused_computation.7.clone.1 | convolution fusion | flops 101711872 | bytes 8392709 | tf_op jit(solution)/shard_map/while/body/eval_jaxpr/sj,skl->jkl/dot_general | solution.py:89
  312.0 3.8 fusion.84
  315.8 7.0 %select_add_fusion.2 = f32[8,256,256]{2,0,1:T(8,128)S(1)} fusion(f32[8,256,256]{2,0,1:T(8,128)S(1)} %get-tuple-element.130, f32[16,256,256]{2,1,0:T(8,128)} %fusion.84, pred[]{:T(512)S(6)} %compare.40, f32[16,16,8]{1,2,0:T(8,128)S(1)} %get-tuple-element.137, s32[]{:T(128)} %get-tuple-element.129), kind=kOutput, calls=%fused_computation.7.clone.1 | convolution fusion | flops 101711872 | bytes 8392709 | tf_op jit(solution)/shard_map/while/body/eval_jaxpr/sj,skl->jkl/dot_general | solution.py:89
  322.8 3.8 fusion.84
  326.6 7.0 %select_add_fusion.2 = f32[8,256,256]{2,0,1:T(8,128)S(1)} fusion(f32[8,256,256]{2,0,1:T(8,128)S(1)} %get-tuple-element.130, f32[16,256,256]{2,1,0:T(8,128)} %fusion.84, pred[]{:T(512)S(6)} %compare.40, f32[16,16,8]{1,2,0:T(8,128)S(1)} %get-tuple-element.137, s32[]{:T(128)} %get-tuple-element.129), kind=kOutput, calls=%fused_computation.7.clone.1 | convolution fusion | flops 101711872 | bytes 8392709 | tf_op jit(solution)/shard_map/while/body/eval_jaxpr/sj,skl->jkl/dot_general | solution.py:89
  333.6 1.8 copy.109
  335.4 2.6 select_reduce_fusion
  338.0 1.8 copy.110
  344.4 1.3 copy-done.2
  345.8 93.8 %custom-call.24 = f32[8,128,128]{2,1,0:T(8,128)S(1)} custom-call(f32[8,128,128]{2,1,0:T(8,128)S(1)} %cholesky.231), custom_call_target="Cholesky" | custom-call | tf_op jit(solution)/shard_map/jit(cholesky)/cholesky | solution.py:99
  439.6 78.6 %custom-call.25 = f32[8,1,128,128]{2,3,1,0:T(8,128)S(1)} custom-call(f32[8,1,128,128]{3,2,1,0:T(8,128)S(1)} %select_bitcast_fusion), custom_call_target="InvertDiagBlocksLowerTriangular" | custom-call | tf_op jit(solution)/shard_map/jit(cholesky)/cholesky | solution.py:99
  518.2 1.7 fusion.12
  519.9 1.6 fusion.27
  523.4 2.0 collective-permute-start.1
  525.4 3.0 convolution_subtract_fusion
  528.5 94.6 %custom-call.26 = f32[8,128,128]{2,1,0:T(8,128)S(1)} custom-call(f32[8,128,128]{2,1,0:T(8,128)} %convolution_subtract_fusion), custom_call_target="Cholesky" | custom-call | tf_op jit(solution)/shard_map/jit(cholesky)/cholesky | solution.py:99
  623.1 1.6 fusion.76
  624.7 1.2 collective-permute-start.2
  626.1 3.9 collective-permute-done.2
  630.6 1.2 select_reduce_fusion.4
  632.5 2.7 collective-permute-start.3
  638.4 1.3 cholesky.200
  639.8 2.3 fusion.75
  642.1 5.8 collective-permute-start.4
  648.2 1.8 copy.119
  650.0 1.6 fusion.19
  652.4 11.7 %cholesky.205 = f32[128,128]{1,0:T(8,128)S(1)} custom-call(f32[128,128]{1,0:T(8,128)S(1)} %cholesky.234), custom_call_target="Cholesky" | custom-call | tf_op jit(solution)/shard_map/jit(cholesky)/cholesky | solution.py:115
  664.2 9.8 %custom-call.27 = f32[1,128,128]{1,2,0:T(8,128)S(1)} custom-call(f32[1,128,128]{2,1,0:T(8,128)S(1)} %get-tuple-element.85), custom_call_target="InvertDiagBlocksLowerTriangular" | custom-call | tf_op jit(solution)/shard_map/jit(cholesky)/cholesky | solution.py:115
  674.5 11.7 %cholesky.219 = f32[128,128]{1,0:T(8,128)S(1)} custom-call(f32[128,128]{1,0:T(8,128)S(1)} %convolution_subtract_fusion.1), custom_call_target="Cholesky" | custom-call | tf_op jit(solution)/shard_map/jit(cholesky)/cholesky | solution.py:115
  (101 shorter events, 21.9 us)
Async XLA Ops:
  0.6 7.9 %copy-start = (bf16[512,256]{1,0:T(8,128)(2,1)S(1)}, bf16[512,256]{1,0:T(8,128)(2,1)}, u32[]{:S(2)}) copy-start(bf16[512,256]{1,0:T(8,128)(2,1)} %param.9) | copy-start | bytes 786436
  0.6 6.6 copy-start.6
  96.6 12.4 %copy-start.7 = (s32[1024,16]{0,1:T(8,128)S(1)}, s32[1024,16]{0,1:T(8,128)}, u32[]{:S(2)}) copy-start(s32[1024,16]{0,1:T(8,128)} %param.12) | copy-start | bytes 196612
  96.6 12.7 %copy-start.8 = (s32[1024,16]{0,1:T(8,128)S(1)}, s32[1024,16]{0,1:T(8,128)}, u32[]{:S(2)}) copy-start(s32[1024,16]{0,1:T(8,128)} %param.11) | copy-start | bytes 196612
  96.6 64.4 %all-to-all-start = ((bf16[128,2,32,256]{3,2,1,0:T(8,128)(2,1)}), bf16[128,2,32,256]{3,2,1,0:T(8,128)(2,1)}, u32[]{:S(2)}, u32[]{:S(2)}) async-start(bf16[128,2,32,256]{3,2,1,0:T(8,128)(2,1)} %broadcast_select_fusion), calls=%async_computation | async-start | bytes 8388608 | tf_op jit(solution)/shard_map/all_to_all | solution.py:64
  339.8 1.2 copy-start.3
  341.0 3.1 copy-start.1
  343.6 96.0 %copy-start.9 = (pred[128,128]{1,0:T(8,128)(4,1)S(1)}, pred[128,128]{1,0:T(8,128)(4,1)}, u32[]{:S(2)}) copy-start(pred[128,128]{1,0:T(8,128)(4,1)} %iota_compare_fusion.4) | copy-start | bytes 49156
  343.6 176.3 %collective-permute-start = (f32[256,256]{1,0:T(8,128)}, f32[256,256]{1,0:T(8,128)}, u32[]{:S(2)}, u32[]{:S(2)}) collective-permute-start(f32[256,256]{1,0:T(8,128)} %divide_reduce_fusion), channel_id=1, source_target_pairs={{0,1},{1,0},{2,3},{3,2},{4,5},{5,4},{6,7},{7,6},{8,9},{9,8},{10,11... | collective-permute-start | bytes 786440 | tf_op jit(solution)/shard_map/ppermute | solution.py:10
  344.4 1.3 copy-start.2
  523.4 99.6 %collective-permute-start.1 = (f32[256,256]{1,0:T(8,128)S(1)}, f32[256,256]{1,0:T(8,128)}, u32[]{:S(2)}, u32[]{:S(2)}) collective-permute-start(f32[256,256]{1,0:T(8,128)S(1)} %multiply_divide_fusion.2), channel_id=1, source_target_pairs={{0,2},{1,3},{2,0},{3,1},{4,6},{5,7},{6,4},{7,5},{8,10},{9,11},{10,... | collective-permute-start | bytes 786440 | tf_op jit(solution)/shard_map/ppermute | solution.py:10
  624.7 5.3 collective-permute-start.2
  632.5 7.2 %collective-permute-start.3 = (f32[256,256]{1,0:T(8,128)S(1)}, f32[256,256]{1,0:T(8,128)}, u32[]{:S(2)}, u32[]{:S(2)}) collective-permute-start(f32[256,256]{1,0:T(8,128)S(1)} %multiply_divide_fusion.1), channel_id=1, source_target_pairs={{0,8},{1,9},{2,10},{3,11},{4,12},{5,13},{6,14},{7,15},{8,0},{9,1},... | collective-permute-start | bytes 786440 | tf_op jit(solution)/shard_map/ppermute | solution.py:10
  637.3 2.3 copy-start.5
  638.3 1.4 copy-start.4
  642.1 7.9 %collective-permute-start.4 = (f32[256,256]{1,0:T(8,128)}, f32[256,256]{1,0:T(8,128)}, u32[]{:S(2)}, u32[]{:S(2)}) collective-permute-start(f32[256,256]{1,0:T(8,128)} %fusion.75), channel_id=1, source_target_pairs={{0,16},{16,0},{32,48},{48,32},{64,80},{80,64},{96,112},{112,96},{1... | collective-permute-start | bytes 786440 | tf_op jit(solution)/shard_map/ppermute | solution.py:10
where the time goes:
time: 695 us; the launch traced here: 690 us
  other arithmetic  318 us (46%)
  matrix products  190 us (27%)
  local copies, waits for them, and re-layouts  101 us (15%)
  waiting for transfers between devices  52.7 us (8%)
  starting transfers between devices  24.7 us (4%)
    another operation x10, other arithmetic, local(): leaf_factor = jnp.linalg.cholesky(gram)  268 us
    dot_general x16, matrix products, add_group(): jnp.einsum('sj,skl->jkl', block_weights, slot_grams, precision=lax.Precis...  112 us
    gather x1, local copies, waits for them, and re-layouts, local(): outgoing = correlated[source_leaf[:, None], cycle_pick]  80.9 us
    dot_general x16, matrix products, add_group(): jnp.einsum('srk,srl->skl', block_rows, block_rows, preferred_element_type...  60 us
    all_to_all x1, waiting for transfers between devices, local(): lax.all_to_all(flat_send, ('grp', 'sib'), split_axis=0, concat_axis=0, ti...  48.8 us
    another operation x7, other arithmetic, local(): root_factor = jnp.linalg.cholesky(current)  34.7 us
  transfers between devices with their start and end apart: 6, of which 2 were waited for; matrix products, arithmetic and copies ran while one was open for 41% of the time, Pallas kernels for 0%

commit v1 on v0

v1 whole, which is shorter than its diff:
```python
import functools

import jax
import jax.numpy as jnp
from jax import lax
from jax.experimental import pallas as pl
from jax.experimental.pallas import tpu as pltpu
from jax.sharding import PartitionSpec as P

F32 = jnp.float32
BF16 = jnp.bfloat16
I32 = jnp.int32
MESH = pl.DeviceIdType.MESH
VMEM = pl.BlockSpec(memory_space=pltpu.VMEM)

RANK = 256
LEAF_DEV = 8
CYCLE = 32
N_SIB = 16
DEVICES = 128
TREE = 32


def iota(shape, dim):
    return lax.broadcasted_iota(I32, shape, dim)


def exact_dot(a, b, dims):
    return lax.dot_general(
        a.astype(BF16), b.astype(BF16), (dims, ((), ())), preferred_element_type=F32
    )


def full_dot(a, b, dims):
    return lax.dot_general(
        a, b, (dims, ((), ())), preferred_element_type=F32, precision=lax.Precision.HIGHEST
    )


def own_device():
    return lax.axis_index("grp") * N_SIB + lax.axis_index("sib")


def chain_kernel(t_ref, q_ref, p_ref):
    def scaled(x):
        return x / jnp.max(jnp.abs(x))

    chain = scaled(t_ref[0])
    for level in range(3):
        q_ref[level] = full_dot(chain, chain, ((1,), (1,)))
        chain = full_dot(chain, t_ref[level + 1], ((1,), (0,)))
        if level < 2:
            chain = scaled(chain)
    p_ref[...] = chain


def pack_kernel(dens, kern, tgt, cyc, out, picks, slot_v, slot_s, hot, samples, sem):
    source = pl.program_id(0)
    n_list = 16

    @pl.when(source == 0)
    def _():
        out[...] = jnp.zeros_like(out)
        own = tgt[pl.ds(own_device(), 1), :]
        dest = own // LEAF_DEV
        hits = (iota((DEVICES, 128), 0) == dest).astype(F32)
        upper = (iota((128, 128), 0) < iota((128, 128), 1)).astype(F32)
        before = exact_dot(hits, upper, ((1,), (0,)))
        ahead = jnp.sum(before * hits, axis=0, keepdims=True)
        slot = dest * 2 + ahead.astype(I32)
        slot_v[...] = jnp.broadcast_to(slot, slot_v.shape)
        copy = pltpu.make_async_copy(slot_v, slot_s, sem)
        copy.start()
        which = (iota((1024, 128), 0) == own).astype(F32)
        rows = cyc[...]
        high = exact_dot((rows // 128).astype(F32), which, ((0,), (0,)))
        low = exact_dot((rows % 128).astype(F32), which, ((0,), (0,)))
        picks[...] = high * 128.0 + low
        copy.wait()

    corr = jnp.dot(dens[0], kern[...], preferred_element_type=F32).astype(BF16)
    mine = pltpu.roll(picks[...], lax.rem(128 - n_list * source, 128), 1)
    lon = iota((CYCLE, 512), 1).astype(F32)
    for k in range(n_list):
        hot[CYCLE * k : CYCLE * (k + 1), :] = (
            jnp.broadcast_to(mine[:, k : k + 1], (CYCLE, 512)) == lon
        ).astype(BF16)
    samples[...] = jnp.dot(hot[...], corr, preferred_element_type=F32).astype(BF16)
    for k in range(n_list):
        out[slot_s[0, source * n_list + k]] = samples[CYCLE * k : CYCLE * (k + 1), :]


ORDER = 384


def gram_kernel(arrived, tgt, q_ref, gram, aug, table_v, table_s, chunk, sem):
    me = own_device()
    targets = tgt[...]
    match = (targets // LEAF_DEV == me).astype(F32)
    leaf = (targets % LEAF_DEV).astype(F32) + 1.0
    upper = (iota((128, 128), 0) < iota((128, 128), 1)).astype(F32)
    before = exact_dot(match, upper, ((1,), (0,)))
    ones = jnp.ones((LEAF_DEV, 128), F32)
    named = match * leaf
    first = exact_dot(ones, jnp.where(before < 0.5, named, 0.0), ((1,), (1,)))
    second = exact_dot(ones, jnp.where(before > 0.5, named, 0.0), ((1,), (1,)))
    slot_leaf = jnp.concatenate([first, second], axis=1)
    lane = iota((LEAF_DEV, 256), 1)
    held = (slot_leaf == (iota((LEAF_DEV, 256), 0) + 1).astype(F32)).astype(F32)
    upper2 = (iota((256, 256), 0) < iota((256, 256), 1)).astype(F32)
    rank = exact_dot(held, upper2, ((1,), (0,)))
    count = jnp.sum(held, axis=1, keepdims=True)
    chunks = (count.astype(I32) + 7) // 8
    wide = jnp.broadcast_to(chunks, (LEAF_DEV, 128)).astype(F32)
    lower = (iota((LEAF_DEV, LEAF_DEV), 1) < iota((LEAF_DEV, LEAF_DEV), 0)).astype(F32)
    start = exact_dot(lower, wide, ((1,), (0,)))
    start2 = jnp.concatenate([start, start], axis=1) * 8.0
    place = jnp.sum(held * (start2 + rank + 1.0), axis=0, keepdims=True) - 1.0
    onto = (iota((ORDER, 256), 0).astype(F32) == place).astype(F32)
    value = (2 * (lane % 128) + lane // 128 + 1).astype(F32)
    order = exact_dot(value, onto, ((1,), (1,))).astype(I32) - 1
    table_v[0:8, :] = order
    table_v[8:16, 0:128] = jnp.broadcast_to(chunks, (LEAF_DEV, 128))
    table_v[16:24, 0:128] = start.astype(I32)
    copy = pltpu.make_async_copy(table_v, table_s, sem)
    copy.start()
    gram[...] = jnp.zeros_like(gram)
    copy.wait()

    most = table_s[8, 0]
    for j in range(1, LEAF_DEV):
        most = jnp.maximum(most, table_s[8 + j, 0])

    def add_chunk(c, carry):
        for j in range(LEAF_DEV):
            inside = c < table_s[8 + j, 0]
            base = jnp.where(inside, (table_s[16 + j, 0] + c) * 8, 0)
            for b in range(8):
                index = table_s[0, base + b]
                live = jnp.logical_and(inside, index >= 0)
                block = arrived[jnp.maximum(index, 0)]
                chunk[j, CYCLE * b : CYCLE * (b + 1), :] = jnp.where(
                    live, block, jnp.zeros_like(block)
                )
        for j in range(LEAF_DEV):
            rows = chunk[j]
            gram[j] = gram[j] + lax.dot_general(
                rows, rows, (((0,), (0,)), ((), ())), preferred_element_type=F32
            )
        return carry

    lax.fori_loop(0, most, add_chunk, 0)

    row = iota((RANK, RANK), 0)
    col = iota((RANK, RANK), 1)
    eye = (row == col).astype(F32)

    def total(x):
        return jnp.sum(jnp.sum(x, axis=0, keepdims=True), axis=1, keepdims=True)

    whole = None
    for node in range(2):
        merged = None
        for child in range(4):
            j = 4 * node + child
            one = gram[j] * (1.0 / CYCLE) + eye
            gram[j] = one
            scaled = one * (RANK / total(one * eye))
            merged = scaled if merged is None else merged + scaled
        scaled = merged * (RANK / total(merged * q_ref[0]))
        whole = scaled if whole is None else whole + scaled
    aug[:, 0:RANK] = whole
    second_trace = total(whole * q_ref[1])
    third_trace = total(whole * q_ref[2])
    aug[:, RANK : RANK + 128] = jnp.where(
        iota((RANK, 128), 0) % 2 == 0, second_trace, third_trace
    )


def tree_kernel(aug, p_ref, root, first, second, part, send_a, recv_a, send_b, recv_b, local):
    grp = lax.axis_index("grp")
    sib = lax.axis_index("sib")
    base = (grp // 2) * 2
    me = (grp % 2) * N_SIB + sib

    def device(index):
        return (base + index // N_SIB, index % N_SIB)

    barrier = pltpu.get_barrier_semaphore()

    def greet(k, carry):
        pl.semaphore_signal(
            barrier, inc=1, device_id=device((me + k) % TREE), device_id_type=MESH
        )
        return carry

    lax.fori_loop(1, TREE, greet, 0)
    pl.semaphore_wait(barrier, TREE - 1)

    def rows_copy(k, target, source):
        return pltpu.make_async_remote_copy(
            src_ref=aug.at[pl.ds(pl.multiple_of(target * 8, 8), 8), :],
            dst_ref=first.at[source],
            send_sem=send_a.at[k],
            recv_sem=recv_a.at[k],
            device_id=device(target),
            device_id_type=MESH,
        )

    def part_copy(k, target, source):
        return pltpu.make_async_remote_copy(
            src_ref=part,
            dst_ref=second.at[pl.ds(pl.multiple_of(source * 8, 8), 8), :],
            send_sem=send_b.at[k],
            recv_sem=recv_b.at[k],
            device_id=device(target),
            device_id_type=MESH,
        )

    def run(make):
        def start(k, carry):
            make(k, (me + k) % TREE, me).start()
            return carry

        lax.fori_loop(1, TREE, start, 0)

    def wait(make):
        def arrive(k, carry):
            make(k, (me + k) % TREE, (me - k + TREE) % TREE).wait_recv()
            return carry

        lax.fori_loop(1, TREE, arrive, 0)

    def drain(make):
        def sent(k, carry):
            make(k, (me + k) % TREE, me).wait_send()
            return carry

        lax.fori_loop(1, TREE, sent, 0)

    run(rows_copy)
    first[me] = aug[pl.ds(pl.multiple_of(me * 8, 8), 8), :]
    wait(rows_copy)

    gathered = None
    for quad in range(4):
        merged = None
        trace = None
        for pair in range(4):
            d = quad * 8 + pair * 2
            both = first[d] + first[d + 1]
            weight = RANK / both[0:1, RANK : RANK + 128]
            third = both[1:2, RANK : RANK + 128] * weight
            weight2 = jnp.concatenate([weight, weight], axis=1)
            scaled = both[:, 0:RANK] * weight2
            merged = scaled if merged is None else merged + scaled
            trace = third if trace is None else trace + third
        weight = RANK / trace
        scaled = merged * jnp.concatenate([weight, weight], axis=1)
        gathered = scaled if gathered is None else gathered + scaled
    part[...] = full_dot(gathered, p_ref[...], ((1,), (0,)))
    run(part_copy)
    second[pl.ds(pl.multiple_of(me * 8, 8), 8), :] = part[...]
    wait(part_copy)
    root[...] = full_dot(p_ref[...], second[...], ((0,), (0,)))
    drain(rows_copy)
    drain(part_copy)


BLOCK = 64


def factor_block(rows):
    n = rows[0].shape[0]
    sub = iota((n, 8, 128), 1)
    for r in range(len(rows)):
        scale = None
        for c in range(8):
            i = 8 * r + c
            cols = [jnp.broadcast_to(x[:, :, i : i + 1], (n, 8, 128)) for x in rows[r:]]
            s = lax.rsqrt(cols[0][:, c : c + 1, :])
            pivot = rows[r][:, c : c + 1, :] * (s * s)
            wide = jnp.broadcast_to(s, (n, 8, 128))
            scale = wide if scale is None else jnp.where(sub >= c, wide, scale)
            if c < 7:
                rows[r] = rows[r] - jnp.where(sub > c, cols[0], 0.0) * pivot
            for q in range(r + 1, len(rows)):
                rows[q] = rows[q] - cols[q - r] * pivot
        rows[r] = rows[r] * scale
    return rows


def cholesky_kernel(gram, root, leaf_out, root_out, work):
    n = LEAF_DEV + 1
    work[0:LEAF_DEV] = gram[...]
    work[LEAF_DEV] = root[...]
    lane = iota((BLOCK, 128), 1)
    eye = (lane - BLOCK == iota((BLOCK, 128), 0)).astype(F32)
    for step in range(RANK // BLOCK):
        r0 = BLOCK * step
        base = 128 * (step // 2)
        odd = step % 2
        block = work[:, r0 : r0 + BLOCK, base : base + 128]
        if odd:
            block = pltpu.roll(block, BLOCK, 2)
        block = jnp.where((lane < BLOCK)[None], block, eye[None])
        rows = factor_block([block[:, 8 * q : 8 * q + 8, :] for q in range(BLOCK // 8)])
        inverse = jnp.concatenate(rows, axis=1)
        if not odd:
            inverse = pltpu.roll(inverse, BLOCK, 2)
        inverse = jnp.where(((lane >= BLOCK) if odd else (lane < BLOCK))[None], inverse, 0.0)
        height = RANK - r0
        below = iota((height, BLOCK), 0) >= iota((height, BLOCK), 1)
        for m in range(n):
            panel = full_dot(work[m, r0:, base : base + 128], inverse[m], ((1,), (1,)))
            panel = jnp.where(below, panel, 0.0)
            out = leaf_out.at[m] if m < LEAF_DEV else root_out.at[0]
            if r0:
                out[0:r0, r0 : r0 + BLOCK] = jnp.zeros((r0, BLOCK), F32)
            out[r0:, r0 : r0 + BLOCK] = panel
            if height > BLOCK:
                c0 = 128 * ((step + 1) // 2)
                if c0 >= r0:
                    cols = panel[c0 - r0 :]
                else:
                    cols = jnp.concatenate([jnp.zeros((r0 - c0, BLOCK), F32), panel], axis=0)
                work[m, r0 + BLOCK :, c0:] = work[m, r0 + BLOCK :, c0:] - full_dot(
                    panel[BLOCK:], cols, ((1,), (1,))
                )


def sds(shape, dtype):
    return jax.ShapeDtypeStruct(shape, dtype)


def local(density, kernel, transfer, target_device, target_slot, cycle_rows):
    params = functools.partial(pltpu.CompilerParams, vmem_limit_bytes=48 * 2**20)
    targets = (target_device * LEAF_DEV + target_slot).reshape(DEVICES, 128)
    packed = pl.pallas_call(
        pack_kernel,
        grid=(LEAF_DEV,),
        out_shape=sds((2 * DEVICES, CYCLE, RANK), BF16),
        in_specs=[
            pl.BlockSpec((1, 512, 512), lambda s: (s, 0, 0)),
            pl.BlockSpec((512, RANK), lambda s: (0, 0)),
            pl.BlockSpec((DEVICES, 128), lambda s: (0, 0)),
            pl.BlockSpec((1024, CYCLE), lambda s: (0, 0)),
        ],
        out_specs=pl.BlockSpec((2 * DEVICES, CYCLE, RANK), lambda s: (0, 0, 0)),
        scratch_shapes=[
            pltpu.VMEM((CYCLE, 128), F32),
            pltpu.VMEM((8, 128), I32),
            pltpu.SMEM((8, 128), I32),
            pltpu.VMEM((512, 512), BF16),
            pltpu.VMEM((512, RANK), BF16),
            pltpu.SemaphoreType.DMA,
        ],
        compiler_params=params(),
        name="pack",
    )(density, kernel, targets, cycle_rows)
    arrived = lax.all_to_all(
        packed.reshape(DEVICES, 2, CYCLE, RANK),
        ("grp", "sib"),
        split_axis=0,
        concat_axis=0,
        tiled=True,
    ).reshape(2 * DEVICES, CYCLE, RANK)
    squares, chain = pl.pallas_call(
        chain_kernel,
        out_shape=(sds((3, RANK, RANK), F32), sds((RANK, RANK), F32)),
        in_specs=[VMEM],
        out_specs=(VMEM, VMEM),
        compiler_params=params(),
        cost_estimate=pl.CostEstimate(
            flops=6 * 6 * 2 * RANK**3, bytes_accessed=8 * 4 * RANK**2, transcendentals=0
        ),
        name="chain",
    )(transfer)
    gram, augmented = pl.pallas_call(
        gram_kernel,
        out_shape=(sds((LEAF_DEV, RANK, RANK), F32), sds((RANK, RANK + 128), F32)),
        in_specs=[VMEM] * 3,
        out_specs=(VMEM, VMEM),
        scratch_shapes=[
            pltpu.VMEM((24, ORDER), I32),
            pltpu.SMEM((24, ORDER), I32),
            pltpu.VMEM((LEAF_DEV, 256, RANK), BF16),
            pltpu.SemaphoreType.DMA,
        ],
        compiler_params=params(),
        name="gram",
    )(arrived, targets, squares)
    root = pl.pallas_call(
        tree_kernel,
        out_shape=sds((RANK, RANK), F32),
        in_specs=[VMEM] * 2,
        out_specs=VMEM,
        scratch_shapes=[
            pltpu.VMEM((TREE, 8, RANK + 128), F32),
            pltpu.VMEM((RANK, RANK), F32),
            pltpu.VMEM((8, RANK), F32),
            pltpu.SemaphoreType.DMA((TREE,)),
            pltpu.SemaphoreType.DMA((TREE,)),
            pltpu.SemaphoreType.DMA((TREE,)),
            pltpu.SemaphoreType.DMA((TREE,)),
            pltpu.SemaphoreType.DMA,
        ],
        compiler_params=params(collective_id=1, has_side_effects=True),
        name="tree",
    )(augmented, chain)
    return pl.pallas_call(
        cholesky_kernel,
        out_shape=(sds((LEAF_DEV, RANK, RANK), F32), sds((1, RANK, RANK), F32)),
        in_specs=[VMEM] * 2,
        out_specs=(VMEM, VMEM),
        scratch_shapes=[pltpu.VMEM((LEAF_DEV + 1, RANK, RANK), F32)],
        compiler_params=params(),
        name="cholesky",
    )(gram, root)


def solution(mesh):
    return jax.shard_map(
        local,
        mesh=mesh,
        in_specs=(P(("grp", "sib"), None, None), P(), P(), P(), P(), P()),
        out_specs=(P(("grp", "sib"), None, None), P(("grp", "sib"), None, None)),
        check_vma=False,
    )
```

time: 695 us -> 139 us (0.20)
  other arithmetic: 318 us -> 0.88 us
  matrix products: 190 us -> 0 us
  local copies, waits for them, and re-layouts: 101 us -> 4.4 us
  Pallas kernels: 0 us -> 70.3 us
  starting transfers between devices: 24.7 us -> 12 us
    another operation x19 -> x0, other arithmetic: 303 us -> none  [the longest x10 268 us: local(): leaf_factor = jnp.linalg.cholesky(gram)]
    dot_general x42 -> x0, matrix products: 185 us -> none  [the longest x16 112 us: add_group(): jnp.einsum('sj,skl->jkl', block_weights, slot_grams, precision=lax.Precis...]
    gather x4 -> x0, local copies, waits for them, and re-layouts: 85.4 us -> none  [the longest x1 80.9 us: local(): outgoing = correlated[source_leaf[:, None], cycle_pick]]
    pallas_call x0 -> x5, Pallas kernels: none -> 70.3 us  [the longest x1 30.2 us: local(): pl.pallas_call(cholesky_kernel, out_shape=(sds((LEAF_DEV, RANK, RANK), F3...]
    ppermute x5 -> x0, starting transfers between devices: 12.2 us -> none  [from_partner(): return lax.ppermute(value, axis, pairs)]
  transfers between devices with their start and end apart: 6 -> 1, of which waited for: 2 -> 1; matrix products, arithmetic and copies ran while one was open for 41% -> 0% of each run, Pallas kernels for 0% -> 2%
where the time goes in v1:
time: 139 us; the launch traced here: 138 us
  Pallas kernels  70.3 us (51%)
  waiting for transfers between devices  49.8 us (36%)
  starting transfers between devices  12 us (9%)
  local copies, waits for them, and re-layouts  4.4 us (3%)
    all_to_all x1, waiting for transfers between devices, local(): lax.all_to_all(packed.reshape(DEVICES, 2, CYCLE, RANK), ('grp', 'sib'), s...  49.8 us
    pallas_call x1, Pallas kernels, local(): pl.pallas_call(cholesky_kernel, out_shape=(sds((LEAF_DEV, RANK, RANK), F3...  30.2 us
    pallas_call x1, Pallas kernels, local(): pl.pallas_call(tree_kernel, out_shape=sds((RANK, RANK), F32), in_specs=[V...  20.2 us
    all_to_all x1, starting transfers between devices, local(): lax.all_to_all(packed.reshape(DEVICES, 2, CYCLE, RANK), ('grp', 'sib'), s...  12 us
    pallas_call x1, Pallas kernels, local(): pl.pallas_call(pack_kernel, grid=(LEAF_DEV,), out_shape=sds((2 * DEVICES,...  9.46 us
    pallas_call x1, Pallas kernels, local(): pl.pallas_call(gram_kernel, out_shape=(sds((LEAF_DEV, RANK, RANK), F32),...  8.4 us
    unnamed x7, local copies, waits for them, and re-layouts  4.02 us
  transfers between devices with their start and end apart: 1, of which 1 were waited for; matrix products, arithmetic and copies ran while one was open for 0% of the time, Pallas kernels for 2%

profile of v1, /device:TPU:1, one launch (start us, length us, event | category | flops | bytes accessed | tf_op | source)
XLA Modules:
  0.0 138.1 jit_solution(5073442418461984331)
XLA Ops:
  0.6 0.9 multiply_add_fusion
  1.5 0.2 copy.10
  1.7 0.2 reshape.13.tgt
  1.9 1.1 copy.11.cyc
  3.0 0.0 copy-start.1
  3.0 0.9 copy-done.1
  4.0 9.5 %pack.1 = bf16[256,32,256]{2,1,0:T(8,128)(2,1)S(1)} custom-call(bf16[8,512,512]{2,1,0:T(8,128)(2,1)} %dens.1, bf16[512,256]{1,0:T(8,128)(2,1)S(1)} %copy-done.1, s32[128,128]{1,0:T(8,128)S(1)} %reshape.13.tgt, s32[1024,32]{1,0:T(8,128)S(1)} %copy.11.cyc), custom_call_target="tpu_custom_call" | custom-call | tf_op jit(solution)/shard_map/pack/pallas_call | solution.py:339
  13.4 0.0 copy-start
  13.5 2.0 %copy-done = bf16[256,32,256]{2,1,0:T(8,128)(2,1)} copy-done((bf16[256,32,256]{2,1,0:T(8,128)(2,1)}, bf16[256,32,256]{2,1,0:T(8,128)(2,1)S(1)}, u32[]{:S(2)}) %copy-start) | copy-done | bytes 4194328
  15.4 0.0 copy-start.2
  15.4 12.0 %all-to-all-start = ((bf16[128,2,32,256]{3,2,1,0:T(8,128)(2,1)}), bf16[128,2,32,256]{3,2,1,0:T(8,128)(2,1)}, u32[]{:S(2)}, u32[]{:S(2)}) async-start(bf16[128,2,32,256]{3,2,1,0:T(8,128)(2,1)} %bitcast.2), calls=%async_computation | async-start | bytes 8388608 | tf_op jit(solution)/shard_map/all_to_all | solution.py:361
  27.4 0.0 copy-done.2
  27.4 2.1 %chain.1 = (f32[3,256,256]{2,1,0:T(8,128)S(1)}, f32[256,256]{1,0:T(8,128)S(1)}) custom-call(f32[4,256,256]{2,1,0:T(8,128)S(1)} %copy-done.2), custom_call_target="tpu_custom_call" | custom-call | flops 1207959552 | bytes 2097152 | tf_op jit(solution)/shard_map/chain/pallas_call | solution.py:368
  29.5 49.8 %all-to-all-done = bf16[128,2,32,256]{3,2,1,0:T(8,128)(2,1)} async-done(((bf16[128,2,32,256]{3,2,1,0:T(8,128)(2,1)}), bf16[128,2,32,256]{3,2,1,0:T(8,128)(2,1)}, u32[]{:S(2)}, u32[]{:S(2)}) %all-to-all-start) | async-done | bytes 4194336 | tf_op jit(solution)/shard_map/all_to_all | solution.py:361
  79.4 8.4 %gram.1 = (f32[8,256,256]{2,1,0:T(8,128)S(1)}, f32[256,384]{1,0:T(8,128)S(1)}) custom-call(bf16[256,32,256]{2,1,0:T(8,128)(2,1)} %bitcast.1.arrived, s32[128,128]{1,0:T(8,128)S(1)} %reshape.13.tgt, f32[3,256,256]{2,1,0:T(8,128)S(1)} %get-tuple-element.6.q_ref), custom_call_target="tpu_custom_call" | custom-call | tf_op jit(solution)/shard_map/gram/pallas_call | solution.py:379
  87.8 20.2 %tree.1.root = f32[256,256]{1,0:T(8,128)S(1)} custom-call(f32[256,384]{1,0:T(8,128)S(1)} %get-tuple-element.8.aug, f32[256,256]{1,0:T(8,128)S(1)} %get-tuple-element.9.p_ref), custom_call_target="tpu_custom_call" | custom-call | tf_op jit(solution)/shard_map/tree/pallas_call | solution.py:393
  108.0 30.2 %cholesky.1 = (f32[8,256,256]{2,1,0:T(8,128)}, f32[1,256,256]{2,1,0:T(8,128)}) custom-call(f32[8,256,256]{2,1,0:T(8,128)S(1)} %get-tuple-element.7.gram, f32[256,256]{1,0:T(8,128)S(1)} %tree.1.root), custom_call_target="tpu_custom_call" | custom-call | tf_op jit(solution)/shard_map/cholesky/pallas_call | solution.py:411
Async XLA Ops:
  3.0 1.0 copy-start.1
  13.4 2.0 %copy-start = (bf16[256,32,256]{2,1,0:T(8,128)(2,1)}, bf16[256,32,256]{2,1,0:T(8,128)(2,1)S(1)}, u32[]{:S(2)}) copy-start(bf16[256,32,256]{2,1,0:T(8,128)(2,1)S(1)} %pack.1) | copy-start | bytes 12582916
  15.4 12.0 %copy-start.2 = (f32[4,256,256]{2,1,0:T(8,128)S(1)}, f32[4,256,256]{2,1,0:T(8,128)}, u32[]{:S(2)}) copy-start(f32[4,256,256]{2,1,0:T(8,128)} %t_ref.1) | copy-start | bytes 3145732
  15.4 64.0 %all-to-all-start = ((bf16[128,2,32,256]{3,2,1,0:T(8,128)(2,1)}), bf16[128,2,32,256]{3,2,1,0:T(8,128)(2,1)}, u32[]{:S(2)}, u32[]{:S(2)}) async-start(bf16[128,2,32,256]{3,2,1,0:T(8,128)(2,1)} %bitcast.2), calls=%async_computation | async-start | bytes 8388608 | tf_op jit(solution)/shard_map/all_to_all | solution.py:361

commit v2 on v1

--- a/solution.py
+++ b/solution.py
@@ -41,20 +41,7 @@
     return lax.axis_index("grp") * N_SIB + lax.axis_index("sib")
 
 
-def chain_kernel(t_ref, q_ref, p_ref):
-    def scaled(x):
-        return x / jnp.max(jnp.abs(x))
-
-    chain = scaled(t_ref[0])
-    for level in range(3):
-        q_ref[level] = full_dot(chain, chain, ((1,), (1,)))
-        chain = full_dot(chain, t_ref[level + 1], ((1,), (0,)))
-        if level < 2:
-            chain = scaled(chain)
-    p_ref[...] = chain
-
-
-def pack_kernel(dens, kern, tgt, cyc, out, picks, slot_v, slot_s, hot, samples, sem):
+def pack_kernel(dens, kern, tgt, cyc, out, owners, picks, slot_v, slot_s, hot, samples, sem):
     source = pl.program_id(0)
     n_list = 16
 
@@ -76,6 +63,13 @@
         high = exact_dot((rows // 128).astype(F32), which, ((0,), (0,)))
         low = exact_dot((rows % 128).astype(F32), which, ((0,), (0,)))
         picks[...] = high * 128.0 + low
+        targets = tgt[...]
+        match = (targets // LEAF_DEV == own_device()).astype(F32)
+        earlier = exact_dot(match, upper, ((1,), (0,)))
+        named = match * ((targets % LEAF_DEV).astype(F32) + 1.0)
+        first = jnp.sum(jnp.where(earlier < 0.5, named, 0.0), axis=1, keepdims=True)
+        second = jnp.sum(jnp.where(earlier > 0.5, named, 0.0), axis=1, keepdims=True)
+        owners[...] = jnp.where(iota((DEVICES, 128), 1) % 64 < CYCLE, first, second)
         copy.wait()
 
     corr = jnp.dot(dens[0], kern[...], preferred_element_type=F32).astype(BF16)
@@ -90,70 +84,107 @@
         out[slot_s[0, source * n_list + k]] = samples[CYCLE * k : CYCLE * (k + 1), :]
 
 
-ORDER = 384
-
-
-def gram_kernel(arrived, tgt, q_ref, gram, aug, table_v, table_s, chunk, sem):
-    me = own_device()
-    targets = tgt[...]
-    match = (targets // LEAF_DEV == me).astype(F32)
-    leaf = (targets % LEAF_DEV).astype(F32) + 1.0
-    upper = (iota((128, 128), 0) < iota((128, 128), 1)).astype(F32)
-    before = exact_dot(match, upper, ((1,), (0,)))
-    ones = jnp.ones((LEAF_DEV, 128), F32)
-    named = match * leaf
-    first = exact_dot(ones, jnp.where(before < 0.5, named, 0.0), ((1,), (1,)))
-    second = exact_dot(ones, jnp.where(before > 0.5, named, 0.0), ((1,), (1,)))
-    slot_leaf = jnp.concatenate([first, second], axis=1)
-    lane = iota((LEAF_DEV, 256), 1)
-    held = (slot_leaf == (iota((LEAF_DEV, 256), 0) + 1).astype(F32)).astype(F32)
-    upper2 = (iota((256, 256), 0) < iota((256, 256), 1)).astype(F32)
-    rank = exact_dot(held, upper2, ((1,), (0,)))
-    count = jnp.sum(held, axis=1, keepdims=True)
-    chunks = (count.astype(I32) + 7) // 8
-    wide = jnp.broadcast_to(chunks, (LEAF_DEV, 128)).astype(F32)
-    lower = (iota((LEAF_DEV, LEAF_DEV), 1) < iota((LEAF_DEV, LEAF_DEV), 0)).astype(F32)
-    start = exact_dot(lower, wide, ((1,), (0,)))
-    start2 = jnp.concatenate([start, start], axis=1) * 8.0
-    place = jnp.sum(held * (start2 + rank + 1.0), axis=0, keepdims=True) - 1.0
-    onto = (iota((ORDER, 256), 0).astype(F32) == place).astype(F32)
-    value = (2 * (lane % 128) + lane // 128 + 1).astype(F32)
-    order = exact_dot(value, onto, ((1,), (1,))).astype(I32) - 1
-    table_v[0:8, :] = order
-    table_v[8:16, 0:128] = jnp.broadcast_to(chunks, (LEAF_DEV, 128))
-    table_v[16:24, 0:128] = start.astype(I32)
-    copy = pltpu.make_async_copy(table_v, table_s, sem)
-    copy.start()
-    gram[...] = jnp.zeros_like(gram)
-    copy.wait()
-
-    most = table_s[8, 0]
-    for j in range(1, LEAF_DEV):
-        most = jnp.maximum(most, table_s[8 + j, 0])
-
-    def add_chunk(c, carry):
-        for j in range(LEAF_DEV):
-            inside = c < table_s[8 + j, 0]
-            base = jnp.where(inside, (table_s[16 + j, 0] + c) * 8, 0)
-            for b in range(8):
-                index = table_s[0, base + b]
-                live = jnp.logical_and(inside, index >= 0)
-                block = arrived[jnp.maximum(index, 0)]
-                chunk[j, CYCLE * b : CYCLE * (b + 1), :] = jnp.where(
-                    live, block, jnp.zeros_like(block)
-                )
-        for j in range(LEAF_DEV):
-            rows = chunk[j]
-            gram[j] = gram[j] + lax.dot_general(
-                rows, rows, (((0,), (0,)), ((), ())), preferred_element_type=F32
+ROUNDS = 16
+PER_ROUND = 8
+
+
+def exchange_kernel(
+    packed, owners, t_ref, gram, root,
+    arrived, sums, q_ref, p_ref, aug, first, second, part,
+    send_x, recv_x, send_a, recv_a, send_b, recv_b, local,
+):
+    grp = lax.axis_index("grp")
+    sib = lax.axis_index("sib")
+    my_x, my_c = grp // 2, grp % 2
+    my_y, my_z = sib // 4, sib % 4
+
+    def place(it, lane, sign):
+        dz, dc = lane // 2, lane % 2
+        dy = (it + dz) % 4
+        dx = (it // 4 + dy) % 4
+        x = (my_x + sign * dx + 4) % 4
+        y = (my_y + sign * dy + 4) % 4
+        z = (my_z + sign * dz + 4) % 4
+        return x * 2 + (my_c + dc) % 2, y * 4 + z
+
+    def each(it, act):
+        @pl.when(it > 0)
+        def _():
+            act(it, 0)
+
+        for lane in range(1, PER_ROUND):
+            act(it, lane)
+
+    def rounds(act):
+        def body(it, carry):
+            each(it, act)
+            return carry
+
+        lax.fori_loop(0, ROUNDS, body, 0)
+
+    barrier = pltpu.get_barrier_semaphore()
+
+    def greet(it, lane):
+        pl.semaphore_signal(barrier, inc=1, device_id=place(it, lane, 1), device_id_type=MESH)
+
+    rounds(greet)
+    pl.semaphore_wait(barrier, DEVICES - 1)
+
+    def block_copy(it, lane):
+        to = place(it, lane, 1)
+        k = it * PER_ROUND + lane
+        return pltpu.make_async_remote_copy(
+            src_ref=packed.at[to[0] * N_SIB + to[1]],
+            dst_ref=arrived.at[k],
+            send_sem=send_x.at[k],
+            recv_sem=recv_x.at[k],
+            device_id=to,
+            device_id_type=MESH,
+        )
+
+    rounds(lambda it, lane: block_copy(it, lane).start())
+    own = pltpu.make_async_copy(packed.at[grp * N_SIB + sib], arrived.at[0], local)
+    own.start()
+
+    def scaled(x):
+        return x / jnp.max(jnp.abs(x))
+
+    chain = scaled(t_ref[0])
+    for level in range(3):
+        q_ref[level] = full_dot(chain, chain, ((1,), (1,)))
+        chain = full_dot(chain, t_ref[level + 1], ((1,), (0,)))
+        if level < 2:
+            chain = scaled(chain)
+    p_ref[...] = chain
+    sums[...] = jnp.zeros_like(sums)
+    own.wait()
+
+    def leaves(it, lane):
+        source = place(it, lane, -1)
+        return owners[pl.ds(source[0] * N_SIB + source[1], 1), :]
+
+    def add_round(it, carry):
+        each(it, lambda i, lane: block_copy(i, lane).wait_recv())
+        low = iota((1, 128), 1) < 64
+        for half in range(2):
+            start = pl.multiple_of(it * PER_ROUND, PER_ROUND) + 4 * half
+            rows = arrived[pl.ds(start, 4)].reshape(4 * 2 * CYCLE, RANK)
+            leaf = jnp.concatenate(
+                [
+                    jnp.where(low, leaves(it, 4 * half + b), leaves(it, 4 * half + b + 1))
+                    for b in (0, 2)
+                ],
+                axis=1,
             )
+            turned = rows.T
+            for j in range(LEAF_DEV):
+                mask = (leaf == float(j + 1)).astype(BF16)
+                sums[j] = sums[j] + jnp.dot(turned * mask, rows, preferred_element_type=F32)
         return carry
 
-    lax.fori_loop(0, most, add_chunk, 0)
-
-    row = iota((RANK, RANK), 0)
-    col = iota((RANK, RANK), 1)
-    eye = (row == col).astype(F32)
+    lax.fori_loop(0, ROUNDS, add_round, 0)
+
+    eye = (iota((RANK, RANK), 0) == iota((RANK, RANK), 1)).astype(F32)
 
     def total(x):
         return jnp.sum(jnp.sum(x, axis=0, keepdims=True), axis=1, keepdims=True)
@@ -163,12 +194,12 @@
         merged = None
         for child in range(4):
             j = 4 * node + child
-            one = gram[j] * (1.0 / CYCLE) + eye
+            one = sums[j] * (1.0 / CYCLE) + eye
             gram[j] = one
-            scaled = one * (RANK / total(one * eye))
-            merged = scaled if merged is None else merged + scaled
-        scaled = merged * (RANK / total(merged * q_ref[0]))
-        whole = scaled if whole is None else whole + scaled
+            weighted = one * (RANK / total(one * eye))
+            merged = weighted if merged is None else merged + weighted
+        weighted = merged * (RANK / total(merged * q_ref[0]))
+        whole = weighted if whole is None else whole + weighted
     aug[:, 0:RANK] = whole
     second_trace = total(whole * q_ref[1])
     third_trace = total(whole * q_ref[2])
@@ -176,26 +207,11 @@
         iota((RANK, 128), 0) % 2 == 0, second_trace, third_trace
     )
 
-
-def tree_kernel(aug, p_ref, root, first, second, part, send_a, recv_a, send_b, recv_b, local):
-    grp = lax.axis_index("grp")
-    sib = lax.axis_index("sib")
     base = (grp // 2) * 2
     me = (grp % 2) * N_SIB + sib
 
     def device(index):
         return (base + index // N_SIB, index % N_SIB)
-
-    barrier = pltpu.get_barrier_semaphore()
-
-    def greet(k, carry):
-        pl.semaphore_signal(
-            barrier, inc=1, device_id=device((me + k) % TREE), device_id_type=MESH
-        )
-        return carry
-
-    lax.fori_loop(1, TREE, greet, 0)
-    pl.semaphore_wait(barrier, TREE - 1)
 
     def rows_copy(k, target, source):
         return pltpu.make_async_remote_copy(
@@ -265,6 +281,7 @@
     root[...] = full_dot(p_ref[...], second[...], ((0,), (0,)))
     drain(rows_copy)
     drain(part_copy)
+    rounds(lambda it, lane: block_copy(it, lane).wait_send())
 
 
 BLOCK = 64
@@ -336,17 +353,20 @@
 def local(density, kernel, transfer, target_device, target_slot, cycle_rows):
     params = functools.partial(pltpu.CompilerParams, vmem_limit_bytes=48 * 2**20)
     targets = (target_device * LEAF_DEV + target_slot).reshape(DEVICES, 128)
-    packed = pl.pallas_call(
+    packed, owners = pl.pallas_call(
         pack_kernel,
         grid=(LEAF_DEV,),
-        out_shape=sds((2 * DEVICES, CYCLE, RANK), BF16),
+        out_shape=(sds((2 * DEVICES, CYCLE, RANK), BF16), sds((DEVICES, 128), F32)),
         in_specs=[
             pl.BlockSpec((1, 512, 512), lambda s: (s, 0, 0)),
             pl.BlockSpec((512, RANK), lambda s: (0, 0)),
             pl.BlockSpec((DEVICES, 128), lambda s: (0, 0)),
             pl.BlockSpec((1024, CYCLE), lambda s: (0, 0)),
         ],
-        out_specs=pl.BlockSpec((2 * DEVICES, CYCLE, RANK), lambda s: (0, 0, 0)),
+        out_specs=(
+            pl.BlockSpec((2 * DEVICES, CYCLE, RANK), lambda s: (0, 0, 0)),
+            pl.BlockSpec((DEVICES, 128), lambda s: (0, 0)),
+        ),
         scratch_shapes=[
             pltpu.VMEM((CYCLE, 128), F32),
             pltpu.VMEM((8, 128), I32),
@@ -358,47 +378,22 @@
         compiler_params=params(),
         name="pack",
     )(density, kernel, targets, cycle_rows)
-    arrived = lax.all_to_all(
-        packed.reshape(DEVICES, 2, CYCLE, RANK),
-        ("grp", "sib"),
-        split_axis=0,
-        concat_axis=0,
-        tiled=True,
-    ).reshape(2 * DEVICES, CYCLE, RANK)
-    squares, chain = pl.pallas_call(
-        chain_kernel,
-        out_shape=(sds((3, RANK, RANK), F32), sds((RANK, RANK), F32)),
-        in_specs=[VMEM],
-        out_specs=(VMEM, VMEM),
-        compiler_params=params(),
-        cost_estimate=pl.CostEstimate(
-            flops=6 * 6 * 2 * RANK**3, bytes_accessed=8 * 4 * RANK**2, transcendentals=0
-        ),
-        name="chain",
-    )(transfer)
-    gram, augmented = pl.pallas_call(
-        gram_kernel,
-        out_shape=(sds((LEAF_DEV, RANK, RANK), F32), sds((RANK, RANK + 128), F32)),
-        in_specs=[VMEM] * 3,
+    gram, root = pl.pallas_call(
+        exchange_kernel,
+        out_shape=(sds((LEAF_DEV, RANK, RANK), F32), sds((RANK, RANK), F32)),
+        in_specs=[pl.BlockSpec(memory_space=pl.ANY), VMEM, VMEM],
         out_specs=(VMEM, VMEM),
         scratch_shapes=[
-            pltpu.VMEM((24, ORDER), I32),
-            pltpu.SMEM((24, ORDER), I32),
-            pltpu.VMEM((LEAF_DEV, 256, RANK), BF16),
-            pltpu.SemaphoreType.DMA,
-        ],
-        compiler_params=params(),
-        name="gram",
-    )(arrived, targets, squares)
-    root = pl.pallas_call(
-        tree_kernel,
-        out_shape=sds((RANK, RANK), F32),
-        in_specs=[VMEM] * 2,
-        out_specs=VMEM,
-        scratch_shapes=[
+            pltpu.VMEM((DEVICES, 2, CYCLE, RANK), BF16),
+            pltpu.VMEM((LEAF_DEV, RANK, RANK), F32),
+            pltpu.VMEM((3, RANK, RANK), F32),
+            pltpu.VMEM((RANK, RANK), F32),
+            pltpu.VMEM((RANK, RANK + 128), F32),
             pltpu.VMEM((TREE, 8, RANK + 128), F32),
             pltpu.VMEM((RANK, RANK), F32),
             pltpu.VMEM((8, RANK), F32),
+            pltpu.SemaphoreType.DMA((DEVICES,)),
+            pltpu.SemaphoreType.DMA((DEVICES,)),
             pltpu.SemaphoreType.DMA((TREE,)),
             pltpu.SemaphoreType.DMA((TREE,)),
             pltpu.SemaphoreType.DMA((TREE,)),
@@ -406,8 +401,8 @@
             pltpu.SemaphoreType.DMA,
         ],
         compiler_params=params(collective_id=1, has_side_effects=True),
-        name="tree",
-    )(augmented, chain)
+        name="exchange",
+    )(packed.reshape(DEVICES, 2, CYCLE, RANK), owners, transfer)
     return pl.pallas_call(
         cholesky_kernel,
         out_shape=(sds((LEAF_DEV, RANK, RANK), F32), sds((1, RANK, RANK), F32)),

time: 139 us -> 132 us (0.950)
  Pallas kernels: 70.3 us -> 125 us
  waiting for transfers between devices: 49.8 us -> 0 us
  starting transfers between devices: 12 us -> 0 us
    pallas_call x4 -> x2, Pallas kernels: 40.2 us -> 95.2 us  [the longest x1 85.7 us: local(): pl.pallas_call(exchange_kernel, out_shape=(sds((LEAF_DEV, RANK, RANK), F3...]
    all_to_all x1 -> x0, waiting for transfers between devices: 49.8 us -> none  [local(): lax.all_to_all(packed.reshape(DEVICES, 2, CYCLE, RANK), ('grp', 'sib'), s...]
    all_to_all x1 -> x0, starting transfers between devices: 12 us -> none  [local(): lax.all_to_all(packed.reshape(DEVICES, 2, CYCLE, RANK), ('grp', 'sib'), s...]
  transfers between devices with their start and end apart: 1 -> 0, of which waited for: 1 -> 0; matrix products, arithmetic and copies ran while one was open for 0% -> 0% of each run, Pallas kernels for 2% -> 0%
where the time goes in v2:
time: 132 us; the launch traced here: 131 us
  Pallas kernels  125 us (95%)
  local copies, waits for them, and re-layouts  4.36 us (3%)
    pallas_call x1, Pallas kernels, local(): pl.pallas_call(exchange_kernel, out_shape=(sds((LEAF_DEV, RANK, RANK), F3...  85.7 us
    pallas_call x1, Pallas kernels, local(): pl.pallas_call(cholesky_kernel, out_shape=(sds((LEAF_DEV, RANK, RANK), F3...  30.2 us
    pallas_call x1, Pallas kernels, local(): pl.pallas_call(pack_kernel, grid=(LEAF_DEV,), out_shape=(sds((2 * DEVICES...  9.5 us
    unnamed x7, local copies, waits for them, and re-layouts  3.98 us

profile of v2, /device:TPU:1, one launch (start us, length us, event | category | flops | bytes accessed | tf_op | source)
XLA Modules:
  0.0 131.4 jit_solution(13193766738601630231)
XLA Ops:
  0.6 0.0 copy-start.1
  0.6 1.0 multiply_add_fusion
  1.6 0.2 copy.10
  1.8 0.2 reshape.10.tgt
  2.0 1.1 copy.11.cyc
  3.1 0.0 copy-start.2
  3.1 0.9 copy-done.2
  4.1 9.5 %pack.1 = (bf16[256,32,256]{2,1,0:T(8,128)(2,1)S(1)}, f32[128,128]{1,0:T(8,128)S(1)}) custom-call(bf16[8,512,512]{2,1,0:T(8,128)(2,1)} %dens.1, bf16[512,256]{1,0:T(8,128)(2,1)S(1)} %copy-done.2, s32[128,128]{1,0:T(8,128)S(1)} %reshape.10.tgt, s32[1024,32]{1,0:T(8,128)S(1)} %copy.11.cyc), custom_call_target="tpu_custom_call" | custom-call | tf_op jit(solution)/shard_map/pack/pallas_call | solution.py:356
  13.6 0.0 copy-start
  13.6 1.9 %copy-done = bf16[256,32,256]{2,1,0:T(8,128)(2,1)} copy-done((bf16[256,32,256]{2,1,0:T(8,128)(2,1)}, bf16[256,32,256]{2,1,0:T(8,128)(2,1)S(1)}, u32[]{:S(2)}) %copy-start) | copy-done | bytes 4194328
  15.5 0.0 copy-done.1
  15.5 85.7 %exchange.1 = (f32[8,256,256]{2,1,0:T(8,128)S(1)}, f32[256,256]{1,0:T(8,128)S(1)}) custom-call(bf16[128,2,32,256]{3,2,1,0:T(8,128)(2,1)} %bitcast.1, f32[128,128]{1,0:T(8,128)S(1)} %get-tuple-element.7.owners, f32[4,256,256]{2,1,0:T(8,128)S(1)} %copy-done.1), custom_call_target="tpu_custom_call" | custom-call | tf_op jit(solution)/shard_map/exchange/pallas_call | solution.py:381
  101.2 30.2 %cholesky.1 = (f32[8,256,256]{2,1,0:T(8,128)}, f32[1,256,256]{2,1,0:T(8,128)}) custom-call(f32[8,256,256]{2,1,0:T(8,128)S(1)} %get-tuple-element.8.gram, f32[256,256]{1,0:T(8,128)S(1)} %get-tuple-element.9.root), custom_call_target="tpu_custom_call" | custom-call | tf_op jit(solution)/shard_map/cholesky/pallas_call | solution.py:406
Async XLA Ops:
  0.6 14.9 %copy-start.1 = (f32[4,256,256]{2,1,0:T(8,128)S(1)}, f32[4,256,256]{2,1,0:T(8,128)}, u32[]{:S(2)}) copy-start(f32[4,256,256]{2,1,0:T(8,128)} %t_ref.1) | copy-start | bytes 3145732
  3.1 1.0 copy-start.2
  13.6 1.9 %copy-start = (bf16[256,32,256]{2,1,0:T(8,128)(2,1)}, bf16[256,32,256]{2,1,0:T(8,128)(2,1)S(1)}, u32[]{:S(2)}) copy-start(bf16[256,32,256]{2,1,0:T(8,128)(2,1)S(1)} %get-tuple-element.6) | copy-start | bytes 12582916

commit v3 on v2

--- a/solution.py
+++ b/solution.py
@@ -41,100 +41,145 @@
     return lax.axis_index("grp") * N_SIB + lax.axis_index("sib")
 
 
-def pack_kernel(dens, kern, tgt, cyc, out, owners, picks, slot_v, slot_s, hot, samples, sem):
+def pack_kernel(
+    dens, kern, dev, slot, cyc, out, owners,
+    picks, slot_v, slot_s, hot, samples, zeros, zero_sem, slot_sem, sem,
+):
     source = pl.program_id(0)
     n_list = 16
+    fill = zeros.shape[0]
+
+    def clear(part):
+        return pltpu.make_async_copy(zeros, out.at[pl.ds(part * fill, fill)], zero_sem.at[part])
+
+    slots_down = pltpu.make_async_copy(slot_v, slot_s, slot_sem)
 
     @pl.when(source == 0)
     def _():
-        out[...] = jnp.zeros_like(out)
-        own = tgt[pl.ds(own_device(), 1), :]
-        dest = own // LEAF_DEV
+        zeros[...] = jnp.zeros_like(zeros)
+        for part in range(2 * DEVICES // fill):
+            clear(part).start()
+        me = own_device()
+        lane = iota((1024, 128), 1)
+        row = iota((1024, 128), 0)
+        mine = (row == me * LEAF_DEV + lane % LEAF_DEV).astype(F32)
+        diagonal = iota((n_list, 128), 0) == iota((n_list, 128), 1) // LEAF_DEV
+
+        def own_entries(x):
+            wide = exact_dot(x.astype(F32), mine, ((1,), (0,)))
+            return jnp.sum(jnp.where(diagonal, wide, 0.0), axis=0, keepdims=True).astype(I32)
+
+        dest, leaf = own_entries(dev[...]), own_entries(slot[...])
         hits = (iota((DEVICES, 128), 0) == dest).astype(F32)
-        upper = (iota((128, 128), 0) < iota((128, 128), 1)).astype(F32)
-        before = exact_dot(hits, upper, ((1,), (0,)))
-        ahead = jnp.sum(before * hits, axis=0, keepdims=True)
-        slot = dest * 2 + ahead.astype(I32)
-        slot_v[...] = jnp.broadcast_to(slot, slot_v.shape)
-        copy = pltpu.make_async_copy(slot_v, slot_s, sem)
-        copy.start()
-        which = (iota((1024, 128), 0) == own).astype(F32)
+        earlier = (iota((128, 128), 0) % LEAF_DEV < iota((128, 128), 1) % LEAF_DEV).astype(F32)
+        ahead = jnp.sum(exact_dot(hits, earlier, ((1,), (0,))) * hits, axis=0, keepdims=True)
+        slot_v[...] = jnp.broadcast_to(dest * 2 + ahead.astype(I32), slot_v.shape)
+        slots_down.start()
+        which = (row == dest * LEAF_DEV + leaf).astype(F32)
         rows = cyc[...]
-        high = exact_dot((rows // 128).astype(F32), which, ((0,), (0,)))
-        low = exact_dot((rows % 128).astype(F32), which, ((0,), (0,)))
+        high = exact_dot((rows // 128).astype(F32), which, ((1,), (0,)))
+        low = exact_dot((rows % 128).astype(F32), which, ((1,), (0,)))
         picks[...] = high * 128.0 + low
-        targets = tgt[...]
-        match = (targets // LEAF_DEV == own_device()).astype(F32)
-        earlier = exact_dot(match, upper, ((1,), (0,)))
-        named = match * ((targets % LEAF_DEV).astype(F32) + 1.0)
-        first = jnp.sum(jnp.where(earlier < 0.5, named, 0.0), axis=1, keepdims=True)
-        second = jnp.sum(jnp.where(earlier > 0.5, named, 0.0), axis=1, keepdims=True)
+        match = dev[...] == me
+        named = jnp.sum(jnp.where(match, slot[...] + 1, 0), axis=0, keepdims=True).astype(F32)
+        named = jnp.concatenate(
+            [named[:, 128 * i : 128 * (i + 1)] for i in range(LEAF_DEV)], axis=0
+        )
+        block = jnp.logical_and(
+            iota((128, 128), 0) // LEAF_DEV == iota((128, 128), 1) // LEAF_DEV,
+            iota((128, 128), 0) < iota((128, 128), 1),
+        )
+        before = exact_dot((named > 0.5).astype(F32), block.astype(F32), ((1,), (0,)))
+        here = iota((DEVICES, 128), 1) // LEAF_DEV == iota((DEVICES, 128), 0) % n_list
+
+        def per_device(x):
+            wide = jnp.broadcast_to(x[:, None, :], (LEAF_DEV, n_list, 128)).reshape(DEVICES, 128)
+            return jnp.sum(jnp.where(here, wide, 0.0), axis=1, keepdims=True)
+
+        first = per_device(jnp.where(before < 0.5, named, 0.0))
+        second = per_device(jnp.where(before > 0.5, named, 0.0))
         owners[...] = jnp.where(iota((DEVICES, 128), 1) % 64 < CYCLE, first, second)
-        copy.wait()
 
     corr = jnp.dot(dens[0], kern[...], preferred_element_type=F32).astype(BF16)
-    mine = pltpu.roll(picks[...], lax.rem(128 - n_list * source, 128), 1)
+    turned = pltpu.roll(picks[...], lax.rem(128 - source, 128), 1)
     lon = iota((CYCLE, 512), 1).astype(F32)
     for k in range(n_list):
+        lane = LEAF_DEV * k
         hot[CYCLE * k : CYCLE * (k + 1), :] = (
-            jnp.broadcast_to(mine[:, k : k + 1], (CYCLE, 512)) == lon
+            jnp.broadcast_to(turned[:, lane : lane + 1], (CYCLE, 512)) == lon
         ).astype(BF16)
-    samples[...] = jnp.dot(hot[...], corr, preferred_element_type=F32).astype(BF16)
+    picked = jnp.dot(hot[...], corr, preferred_element_type=F32).astype(BF16)
+    start = pl.multiple_of(source * n_list, n_list)
+    samples[pl.ds(start, n_list)] = picked.reshape(n_list, CYCLE, RANK)
+
+    @pl.when(source == 0)
+    def _():
+        slots_down.wait()
+        for part in range(2 * DEVICES // fill):
+            clear(part).wait()
+
     for k in range(n_list):
-        out[slot_s[0, source * n_list + k]] = samples[CYCLE * k : CYCLE * (k + 1), :]
-
-
+        pltpu.make_async_copy(
+            samples.at[start + k], out.at[slot_s[0, source + LEAF_DEV * k]], sem
+        ).start()
+
+    @pl.when(source == LEAF_DEV - 1)
+    def _():
+        pltpu.make_async_copy(samples, out.at[pl.ds(0, DEVICES)], sem).wait()
+
+
+SWEEP = 32
 ROUNDS = 16
 PER_ROUND = 8
 
 
 def exchange_kernel(
-    packed, owners, t_ref, gram, root,
-    arrived, sums, q_ref, p_ref, aug, first, second, part,
-    send_x, recv_x, send_a, recv_a, send_b, recv_b, local,
+    packed, owners, transfer, gram, root,
+    arrived, sums, t_ref, q_ref, p_ref, aug, first, second, part,
+    send_x, recv_x, send_a, recv_a, send_b, recv_b, local, local_t,
 ):
     grp = lax.axis_index("grp")
     sib = lax.axis_index("sib")
-    my_x, my_c = grp // 2, grp % 2
-    my_y, my_z = sib // 4, sib % 4
-
-    def place(it, lane, sign):
-        dz, dc = lane // 2, lane % 2
-        dy = (it + dz) % 4
-        dx = (it // 4 + dy) % 4
-        x = (my_x + sign * dx + 4) % 4
-        y = (my_y + sign * dy + 4) % 4
-        z = (my_z + sign * dz + 4) % 4
-        return x * 2 + (my_c + dc) % 2, y * 4 + z
-
-    def each(it, act):
-        @pl.when(it > 0)
-        def _():
-            act(it, 0)
-
-        for lane in range(1, PER_ROUND):
-            act(it, lane)
-
-    def rounds(act):
-        def body(it, carry):
-            each(it, act)
+    my_x, my_c = lax.div(grp, 2), lax.rem(grp, 2)
+    my_y, my_z = lax.div(sib, 4), lax.rem(sib, 4)
+    ys = [lax.rem(my_y + d, 4) * 4 for d in range(4)]
+    zs = [lax.rem(my_z + d, 4) for d in range(4)]
+    cs = [my_c, 1 - my_c]
+    other = (my_x * 2 + cs[1], sib)
+
+    def steps(lane):
+        dz, dc = lane // 2 % 4, lane % 2
+        return (lane // 8 + dz) % 4, dz, dc
+
+    def sweeps(act):
+        def body(sweep, carry):
+            xs = [lax.rem(my_x + sweep + d, 4) * 2 for d in range(4)]
+            for lane in range(SWEEP):
+                dy, dz, dc = steps(lane)
+                to = (xs[dy] + cs[dc], ys[dy] + zs[dz])
+                if lane == 0:
+
+                    @pl.when(sweep > 0)
+                    def _():
+                        act(sweep * SWEEP, to)
+
+                else:
+                    act(sweep * SWEEP + lane, to)
             return carry
 
-        lax.fori_loop(0, ROUNDS, body, 0)
+        lax.fori_loop(0, 4, body, 0)
 
     barrier = pltpu.get_barrier_semaphore()
 
-    def greet(it, lane):
-        pl.semaphore_signal(barrier, inc=1, device_id=place(it, lane, 1), device_id_type=MESH)
-
-    rounds(greet)
+    def greet(k, to):
+        pl.semaphore_signal(barrier, inc=1, device_id=to, device_id_type=MESH)
+
+    sweeps(greet)
     pl.semaphore_wait(barrier, DEVICES - 1)
 
-    def block_copy(it, lane):
-        to = place(it, lane, 1)
-        k = it * PER_ROUND + lane
+    def block_copy(k, to, row=0):
         return pltpu.make_async_remote_copy(
-            src_ref=packed.at[to[0] * N_SIB + to[1]],
+            src_ref=packed.at[row],
             dst_ref=arrived.at[k],
             send_sem=send_x.at[k],
             recv_sem=recv_x.at[k],
@@ -142,9 +187,13 @@
             device_id_type=MESH,
         )
 
-    rounds(lambda it, lane: block_copy(it, lane).start())
+    sweeps(lambda k, to: block_copy(k, to, to[0] * N_SIB + to[1]).start())
     own = pltpu.make_async_copy(packed.at[grp * N_SIB + sib], arrived.at[0], local)
     own.start()
+    transfers_in = pltpu.make_async_copy(transfer, t_ref, local_t)
+    transfers_in.start()
+    sums[...] = jnp.zeros_like(sums)
+    transfers_in.wait()
 
     def scaled(x):
         return x / jnp.max(jnp.abs(x))
@@ -156,15 +205,22 @@
         if level < 2:
             chain = scaled(chain)
     p_ref[...] = chain
-    sums[...] = jnp.zeros_like(sums)
     own.wait()
 
     def leaves(it, lane):
-        source = place(it, lane, -1)
-        return owners[pl.ds(source[0] * N_SIB + source[1], 1), :]
+        dy, dz, dc = lax.rem(lax.rem(it, 4) + lane // 2, 4), lane // 2, lane % 2
+        x = lax.rem(my_x + 8 - lax.div(it, 4) - dy, 4)
+        y = lax.rem(my_y + 4 - dy, 4)
+        z = zs[(4 - dz) % 4]
+        return owners[pl.ds((x * 2 + cs[dc]) * N_SIB + y * 4 + z, 1), :]
 
     def add_round(it, carry):
-        each(it, lambda i, lane: block_copy(i, lane).wait_recv())
+        @pl.when(it > 0)
+        def _():
+            block_copy(it * PER_ROUND, other).wait_recv()
+
+        for lane in range(1, PER_ROUND):
+            block_copy(it * PER_ROUND + lane, other).wait_recv()
         low = iota((1, 128), 1) < 64
         for half in range(2):
             start = pl.multiple_of(it * PER_ROUND, PER_ROUND) + 4 * half
@@ -207,56 +263,67 @@
         iota((RANK, 128), 0) % 2 == 0, second_trace, third_trace
     )
 
-    base = (grp // 2) * 2
-    me = (grp % 2) * N_SIB + sib
-
-    def device(index):
-        return (base + index // N_SIB, index % N_SIB)
-
-    def rows_copy(k, target, source):
+    me = my_c * N_SIB + sib
+
+    def around(act):
+        for shift in range(1, TREE):
+            dc, dz, dy = shift % 2, shift // 2 % 4, shift // 8
+            place = (my_x * 2 + cs[dc], ys[dy] + zs[dz])
+            act(shift, place, cs[dc] * N_SIB + place[1])
+
+    def rows_copy(k, to, target):
         return pltpu.make_async_remote_copy(
             src_ref=aug.at[pl.ds(pl.multiple_of(target * 8, 8), 8), :],
-            dst_ref=first.at[source],
+            dst_ref=first.at[me],
             send_sem=send_a.at[k],
             recv_sem=recv_a.at[k],
-            device_id=device(target),
+            device_id=to,
             device_id_type=MESH,
         )
 
-    def part_copy(k, target, source):
+    def part_copy(k, to, target):
         return pltpu.make_async_remote_copy(
             src_ref=part,
-            dst_ref=second.at[pl.ds(pl.multiple_of(source * 8, 8), 8), :],
+            dst_ref=second.at[pl.ds(pl.multiple_of(me * 8, 8), 8), :],
             send_sem=send_b.at[k],
             recv_sem=recv_b.at[k],
-            device_id=device(target),
+            device_id=to,
             device_id_type=MESH,
         )
 
     def run(make):
-        def start(k, carry):
-            make(k, (me + k) % TREE, me).start()
-            return carry
-
-        lax.fori_loop(1, TREE, start, 0)
-
-    def wait(make):
-        def arrive(k, carry):
-            make(k, (me + k) % TREE, (me - k + TREE) % TREE).wait_recv()
-            return carry
-
-        lax.fori_loop(1, TREE, arrive, 0)
+        around(lambda k, to, target: make(k, to, target).start())
+
+    def wait_rows(k, to, target):
+        pltpu.make_async_remote_copy(
+            src_ref=aug.at[0:8, :],
+            dst_ref=first.at[source_rank(k)],
+            send_sem=send_a.at[k],
+            recv_sem=recv_a.at[k],
+            device_id=to,
+            device_id_type=MESH,
+        ).wait_recv()
+
+    def wait_part(k, to, target):
+        pltpu.make_async_remote_copy(
+            src_ref=part,
+            dst_ref=second.at[pl.ds(pl.multiple_of(source_rank(k) * 8, 8), 8), :],
+            send_sem=send_b.at[k],
+            recv_sem=recv_b.at[k],
+            device_id=to,
+            device_id_type=MESH,
+        ).wait_recv()
+
+    def source_rank(shift):
+        dc, dz, dy = shift % 2, shift // 2 % 4, shift // 8
+        return cs[dc] * N_SIB + ys[(4 - dy) % 4] + zs[(4 - dz) % 4]
 
     def drain(make):
-        def sent(k, carry):
-            make(k, (me + k) % TREE, me).wait_send()
-            return carry
-
-        lax.fori_loop(1, TREE, sent, 0)
+        around(lambda k, to, target: make(k, to, target).wait_send())
 
     run(rows_copy)
     first[me] = aug[pl.ds(pl.multiple_of(me * 8, 8), 8), :]
-    wait(rows_copy)
+    around(wait_rows)
 
     gathered = None
     for quad in range(4):
@@ -277,11 +344,16 @@
     part[...] = full_dot(gathered, p_ref[...], ((1,), (0,)))
     run(part_copy)
     second[pl.ds(pl.multiple_of(me * 8, 8), 8), :] = part[...]
-    wait(part_copy)
+    around(wait_part)
     root[...] = full_dot(p_ref[...], second[...], ((0,), (0,)))
     drain(rows_copy)
     drain(part_copy)
-    rounds(lambda it, lane: block_copy(it, lane).wait_send())
+
+    def sent(k, carry):
+        block_copy(k, other).wait_send()
+        return carry
+
+    lax.fori_loop(1, DEVICES, sent, 0)
 
 
 BLOCK = 64
@@ -352,7 +424,6 @@
 
 def local(density, kernel, transfer, target_device, target_slot, cycle_rows):
     params = functools.partial(pltpu.CompilerParams, vmem_limit_bytes=48 * 2**20)
-    targets = (target_device * LEAF_DEV + target_slot).reshape(DEVICES, 128)
     packed, owners = pl.pallas_call(
         pack_kernel,
         grid=(LEAF_DEV,),
@@ -360,11 +431,12 @@
         in_specs=[
             pl.BlockSpec((1, 512, 512), lambda s: (s, 0, 0)),
             pl.BlockSpec((512, RANK), lambda s: (0, 0)),
-            pl.BlockSpec((DEVICES, 128), lambda s: (0, 0)),
-            pl.BlockSpec((1024, CYCLE), lambda s: (0, 0)),
+            pl.BlockSpec((16, 1024), lambda s: (0, 0)),
+            pl.BlockSpec((16, 1024), lambda s: (0, 0)),
+            pl.BlockSpec((CYCLE, 1024), lambda s: (0, 0)),
         ],
         out_specs=(
-            pl.BlockSpec((2 * DEVICES, CYCLE, RANK), lambda s: (0, 0, 0)),
+            pl.BlockSpec(memory_space=pltpu.HBM),
             pl.BlockSpec((DEVICES, 128), lambda s: (0, 0)),
         ),
         scratch_shapes=[
@@ -372,20 +444,24 @@
             pltpu.VMEM((8, 128), I32),
             pltpu.SMEM((8, 128), I32),
             pltpu.VMEM((512, 512), BF16),
-            pltpu.VMEM((512, RANK), BF16),
+            pltpu.VMEM((DEVICES, CYCLE, RANK), BF16),
+            pltpu.VMEM((32, CYCLE, RANK), BF16),
+            pltpu.SemaphoreType.DMA((8,)),
+            pltpu.SemaphoreType.DMA,
             pltpu.SemaphoreType.DMA,
         ],
-        compiler_params=params(),
+        compiler_params=pltpu.CompilerParams(vmem_limit_bytes=62 * 2**20),
         name="pack",
-    )(density, kernel, targets, cycle_rows)
+    )(density, kernel, target_device.T, target_slot.T, cycle_rows.T)
     gram, root = pl.pallas_call(
         exchange_kernel,
         out_shape=(sds((LEAF_DEV, RANK, RANK), F32), sds((RANK, RANK), F32)),
-        in_specs=[pl.BlockSpec(memory_space=pl.ANY), VMEM, VMEM],
+        in_specs=[pl.BlockSpec(memory_space=pl.ANY), VMEM, pl.BlockSpec(memory_space=pl.ANY)],
         out_specs=(VMEM, VMEM),
         scratch_shapes=[
             pltpu.VMEM((DEVICES, 2, CYCLE, RANK), BF16),
             pltpu.VMEM((LEAF_DEV, RANK, RANK), F32),
+            pltpu.VMEM((4, RANK, RANK), F32),
             pltpu.VMEM((3, RANK, RANK), F32),
             pltpu.VMEM((RANK, RANK), F32),
             pltpu.VMEM((RANK, RANK + 128), F32),
@@ -398,6 +474,7 @@
             pltpu.SemaphoreType.DMA((TREE,)),
             pltpu.SemaphoreType.DMA((TREE,)),
             pltpu.SemaphoreType.DMA((TREE,)),
+            pltpu.SemaphoreType.DMA,
             pltpu.SemaphoreType.DMA,
         ],
         compiler_params=params(collective_id=1, has_side_effects=True),

time: 132 us -> 129 us (0.977)
  local copies, waits for them, and re-layouts: 4.36 us -> 0.84 us
  Pallas kernels: 125 us -> 127 us
    unnamed x7 -> x4, local copies, waits for them, and re-layouts: 3.98 us -> 0.84 us
    pallas_call x1, Pallas kernels: 9.5 us -> 11.4 us  [local(): pl.pallas_call(pack_kernel, grid=(LEAF_DEV,), out_shape=(sds((2 * DEVICES...]
where the time goes in v3:
time: 129 us
  Pallas kernels  127 us (98%)
    pallas_call x1, Pallas kernels, local(): pl.pallas_call(exchange_kernel, out_shape=(sds((LEAF_DEV, RANK, RANK), F3...  85.4 us
    pallas_call x1, Pallas kernels, local(): pl.pallas_call(cholesky_kernel, out_shape=(sds((LEAF_DEV, RANK, RANK), F3...  30.2 us
    pallas_call x1, Pallas kernels, local(): pl.pallas_call(pack_kernel, grid=(LEAF_DEV,), out_shape=(sds((2 * DEVICES...  11.4 us

profile of v3, /device:TPU:1, one launch (start us, length us, event | category | flops | bytes accessed | tf_op | source)
XLA Modules:
  0.0 128.5 jit_solution(13873446313780314045)
XLA Ops:
  0.6 0.0 copy-start
  0.6 11.4 %pack.1 = (bf16[256,32,256]{2,1,0:T(8,128)(2,1)}, f32[128,128]{1,0:T(8,128)}) custom-call(bf16[8,512,512]{2,1,0:T(8,128)(2,1)} %dens.1, bf16[512,256]{1,0:T(8,128)(2,1)} %kern.1, s32[16,1024]{1,0:T(8,128)} %bitcast.6, s32[16,1024]{1,0:T(8,128)} %bitcast.7, s32[32,1024]{1,0:T(8,128)} %bitcast.5), custom_call_target="tpu_custom_call" | custom-call | tf_op jit(solution)/shard_map/pack/pallas_call | solution.py:427
  12.0 0.0 copy-done
  12.0 0.0 copy-start.1
  12.0 0.8 copy-done.1
  12.9 85.4 %exchange.1 = (f32[8,256,256]{2,1,0:T(8,128)S(1)}, f32[256,256]{1,0:T(8,128)S(1)}) custom-call(bf16[128,2,32,256]{3,2,1,0:T(8,128)(2,1)} %bitcast.4, f32[128,128]{1,0:T(8,128)S(1)} %copy-done.1, f32[4,256,256]{2,1,0:T(8,128)S(1)} %copy-done), custom_call_target="tpu_custom_call" | custom-call | tf_op jit(solution)/shard_map/exchange/pallas_call | solution.py:456
  98.3 30.2 %cholesky.1 = (f32[8,256,256]{2,1,0:T(8,128)}, f32[1,256,256]{2,1,0:T(8,128)}) custom-call(f32[8,256,256]{2,1,0:T(8,128)S(1)} %get-tuple-element.8.gram, f32[256,256]{1,0:T(8,128)S(1)} %get-tuple-element.9.root), custom_call_target="tpu_custom_call" | custom-call | tf_op jit(solution)/shard_map/cholesky/pallas_call | solution.py:483
Async XLA Ops:
  0.6 11.4 %copy-start = (f32[4,256,256]{2,1,0:T(8,128)S(1)}, f32[4,256,256]{2,1,0:T(8,128)}, u32[]{:S(2)}) copy-start(f32[4,256,256]{2,1,0:T(8,128)} %transfer.1) | copy-start | bytes 3145732
  12.0 0.8 copy-start.1

commit v4 on v3

--- a/solution.py
+++ b/solution.py
@@ -364,17 +364,29 @@
     sub = iota((n, 8, 128), 1)
     for r in range(len(rows)):
         scale = None
-        for c in range(8):
-            i = 8 * r + c
-            cols = [jnp.broadcast_to(x[:, :, i : i + 1], (n, 8, 128)) for x in rows[r:]]
-            s = lax.rsqrt(cols[0][:, c : c + 1, :])
-            pivot = rows[r][:, c : c + 1, :] * (s * s)
-            wide = jnp.broadcast_to(s, (n, 8, 128))
-            scale = wide if scale is None else jnp.where(sub >= c, wide, scale)
-            if c < 7:
-                rows[r] = rows[r] - jnp.where(sub > c, cols[0], 0.0) * pivot
-            for q in range(r + 1, len(rows)):
-                rows[q] = rows[q] - cols[q - r] * pivot
+        left = len(rows) - r
+        group = 4 if left <= 4 else 2
+        for c0 in range(0, 8, group):
+            lanes = range(8 * r + c0, 8 * r + c0 + group)
+            cols = [
+                [jnp.broadcast_to(x[:, :, i : i + 1], (n, 8, 128)) for x in rows[r:]]
+                for i in lanes
+            ]
+            for a in range(group):
+                c = c0 + a
+                s = lax.rsqrt(cols[a][0][:, c : c + 1, :])
+                inverse = s * s
+                pivot = rows[r][:, c : c + 1, :] * inverse
+                for later in cols[a + 1 :]:
+                    share = later[0][:, c : c + 1, :] * inverse
+                    for q in range(left):
+                        later[q] = later[q] - cols[a][q] * share
+                wide = jnp.broadcast_to(s, (n, 8, 128))
+                scale = wide if scale is None else jnp.where(sub >= c, wide, scale)
+                if c < 7:
+                    rows[r] = rows[r] - jnp.where(sub > c, cols[a][0], 0.0) * pivot
+                for q in range(1, left):
+                    rows[r + q] = rows[r + q] - cols[a][q] * pivot
         rows[r] = rows[r] * scale
     return rows
 

time: 129 us -> 119 us (0.922)
  Pallas kernels: 127 us -> 117 us
    pallas_call x1, Pallas kernels: 30.2 us -> 20.1 us  [local(): pl.pallas_call(cholesky_kernel, out_shape=(sds((LEAF_DEV, RANK, RANK), F3...]
where the time goes in v4:
time: 119 us; the launch traced here: 118 us
  Pallas kernels  117 us (98%)
    pallas_call x1, Pallas kernels, local(): pl.pallas_call(exchange_kernel, out_shape=(sds((LEAF_DEV, RANK, RANK), F3...  85.3 us
    pallas_call x1, Pallas kernels, local(): pl.pallas_call(cholesky_kernel, out_shape=(sds((LEAF_DEV, RANK, RANK), F3...  20.1 us
    pallas_call x1, Pallas kernels, local(): pl.pallas_call(pack_kernel, grid=(LEAF_DEV,), out_shape=(sds((2 * DEVICES...  11.4 us

profile of v4, /device:TPU:1, one launch (start us, length us, event | category | flops | bytes accessed | tf_op | source)
XLA Modules:
  0.0 118.2 jit_solution(2326035903607845543)
XLA Ops:
  0.6 0.0 copy-start
  0.6 11.4 %pack.1 = (bf16[256,32,256]{2,1,0:T(8,128)(2,1)}, f32[128,128]{1,0:T(8,128)}) custom-call(bf16[8,512,512]{2,1,0:T(8,128)(2,1)} %dens.1, bf16[512,256]{1,0:T(8,128)(2,1)} %kern.1, s32[16,1024]{1,0:T(8,128)} %bitcast.6, s32[16,1024]{1,0:T(8,128)} %bitcast.7, s32[32,1024]{1,0:T(8,128)} %bitcast.5), custom_call_target="tpu_custom_call" | custom-call | tf_op jit(solution)/shard_map/pack/pallas_call | solution.py:439
  12.0 0.0 copy-done
  12.0 0.0 copy-start.1
  12.0 0.8 copy-done.1
  12.9 85.3 %exchange.1 = (f32[8,256,256]{2,1,0:T(8,128)S(1)}, f32[256,256]{1,0:T(8,128)S(1)}) custom-call(bf16[128,2,32,256]{3,2,1,0:T(8,128)(2,1)} %bitcast.4, f32[128,128]{1,0:T(8,128)S(1)} %copy-done.1, f32[4,256,256]{2,1,0:T(8,128)S(1)} %copy-done), custom_call_target="tpu_custom_call" | custom-call | tf_op jit(solution)/shard_map/exchange/pallas_call | solution.py:468
  98.2 20.1 %cholesky.1 = (f32[8,256,256]{2,1,0:T(8,128)}, f32[1,256,256]{2,1,0:T(8,128)}) custom-call(f32[8,256,256]{2,1,0:T(8,128)S(1)} %get-tuple-element.8.gram, f32[256,256]{1,0:T(8,128)S(1)} %get-tuple-element.9.root), custom_call_target="tpu_custom_call" | custom-call | tf_op jit(solution)/shard_map/cholesky/pallas_call | solution.py:495
Async XLA Ops:
  0.6 11.4 %copy-start = (f32[4,256,256]{2,1,0:T(8,128)S(1)}, f32[4,256,256]{2,1,0:T(8,128)}, u32[]{:S(2)}) copy-start(f32[4,256,256]{2,1,0:T(8,128)} %transfer.1) | copy-start | bytes 3145732
  12.0 0.8 copy-start.1

commit v5 on v4

--- a/solution.py
+++ b/solution.py
@@ -41,11 +41,14 @@
     return lax.axis_index("grp") * N_SIB + lax.axis_index("sib")
 
 
+PER_STEP = 4
+
+
 def pack_kernel(
     dens, kern, dev, slot, cyc, out, owners,
     picks, slot_v, slot_s, hot, samples, zeros, zero_sem, slot_sem, sem,
 ):
-    source = pl.program_id(0)
+    step = pl.program_id(0)
     n_list = 16
     fill = zeros.shape[0]
 
@@ -54,7 +57,7 @@
 
     slots_down = pltpu.make_async_copy(slot_v, slot_s, slot_sem)
 
-    @pl.when(source == 0)
+    @pl.when(step == 0)
     def _():
         zeros[...] = jnp.zeros_like(zeros)
         for part in range(2 * DEVICES // fill):
@@ -100,30 +103,41 @@
         second = per_device(jnp.where(before > 0.5, named, 0.0))
         owners[...] = jnp.where(iota((DEVICES, 128), 1) % 64 < CYCLE, first, second)
 
-    corr = jnp.dot(dens[0], kern[...], preferred_element_type=F32).astype(BF16)
-    turned = pltpu.roll(picks[...], lax.rem(128 - source, 128), 1)
+    corr = jnp.dot(
+        dens[...].reshape(PER_STEP * 512, 512), kern[...], preferred_element_type=F32
+    ).astype(BF16)
     lon = iota((CYCLE, 512), 1).astype(F32)
-    for k in range(n_list):
-        lane = LEAF_DEV * k
-        hot[CYCLE * k : CYCLE * (k + 1), :] = (
-            jnp.broadcast_to(turned[:, lane : lane + 1], (CYCLE, 512)) == lon
+    for sub in range(PER_STEP):
+        source = step * PER_STEP + sub
+        turned = pltpu.roll(picks[...], lax.rem(128 - source, 128), 1)
+        for k in range(n_list):
+            lane = LEAF_DEV * k
+            hot[sub, CYCLE * k : CYCLE * (k + 1), :] = (
+                jnp.broadcast_to(turned[:, lane : lane + 1], (CYCLE, 512)) == lon
+            ).astype(BF16)
+    for sub in range(PER_STEP):
+        picked = jnp.dot(
+            hot[sub], corr[512 * sub : 512 * (sub + 1)], preferred_element_type=F32
         ).astype(BF16)
-    picked = jnp.dot(hot[...], corr, preferred_element_type=F32).astype(BF16)
-    start = pl.multiple_of(source * n_list, n_list)
-    samples[pl.ds(start, n_list)] = picked.reshape(n_list, CYCLE, RANK)
-
-    @pl.when(source == 0)
+        start = pl.multiple_of((step * PER_STEP + sub) * n_list, n_list)
+        samples[pl.ds(start, n_list)] = picked.reshape(n_list, CYCLE, RANK)
+
+    @pl.when(step == 0)
     def _():
         slots_down.wait()
         for part in range(2 * DEVICES // fill):
             clear(part).wait()
 
-    for k in range(n_list):
-        pltpu.make_async_copy(
-            samples.at[start + k], out.at[slot_s[0, source + LEAF_DEV * k]], sem
-        ).start()
-
-    @pl.when(source == LEAF_DEV - 1)
+    for sub in range(PER_STEP):
+        source = step * PER_STEP + sub
+        for k in range(n_list):
+            pltpu.make_async_copy(
+                samples.at[source * n_list + k],
+                out.at[slot_s[0, source + LEAF_DEV * k]],
+                sem,
+            ).start()
+
+    @pl.when(step == LEAF_DEV // PER_STEP - 1)
     def _():
         pltpu.make_async_copy(samples, out.at[pl.ds(0, DEVICES)], sem).wait()
 
@@ -148,8 +162,8 @@
     other = (my_x * 2 + cs[1], sib)
 
     def steps(lane):
-        dz, dc = lane // 2 % 4, lane % 2
-        return (lane // 8 + dz) % 4, dz, dc
+        dz, dc = lane % 4, lane // 16
+        return (lane // 4 + dz) % 4, dz, dc
 
     def sweeps(act):
         def body(sweep, carry):
@@ -208,11 +222,12 @@
     own.wait()
 
     def leaves(it, lane):
-        dy, dz, dc = lax.rem(lax.rem(it, 4) + lane // 2, 4), lane // 2, lane % 2
+        dz = lane % 4
+        dy = lax.rem(lax.rem(it, 4) * 2 + lane // 4 + dz, 4)
         x = lax.rem(my_x + 8 - lax.div(it, 4) - dy, 4)
         y = lax.rem(my_y + 4 - dy, 4)
-        z = zs[(4 - dz) % 4]
-        return owners[pl.ds((x * 2 + cs[dc]) * N_SIB + y * 4 + z, 1), :]
+        core = lax.rem(my_c + lax.div(lax.rem(it, 4), 2), 2)
+        return owners[pl.ds((x * 2 + core) * N_SIB + y * 4 + zs[(4 - dz) % 4], 1), :]
 
     def add_round(it, carry):
         @pl.when(it > 0)
@@ -438,10 +453,10 @@
     params = functools.partial(pltpu.CompilerParams, vmem_limit_bytes=48 * 2**20)
     packed, owners = pl.pallas_call(
         pack_kernel,
-        grid=(LEAF_DEV,),
+        grid=(LEAF_DEV // PER_STEP,),
         out_shape=(sds((2 * DEVICES, CYCLE, RANK), BF16), sds((DEVICES, 128), F32)),
         in_specs=[
-            pl.BlockSpec((1, 512, 512), lambda s: (s, 0, 0)),
+            pl.BlockSpec((PER_STEP, 512, 512), lambda s: (s, 0, 0)),
             pl.BlockSpec((512, RANK), lambda s: (0, 0)),
             pl.BlockSpec((16, 1024), lambda s: (0, 0)),
             pl.BlockSpec((16, 1024), lambda s: (0, 0)),
@@ -455,7 +470,7 @@
             pltpu.VMEM((CYCLE, 128), F32),
             pltpu.VMEM((8, 128), I32),
             pltpu.SMEM((8, 128), I32),
-            pltpu.VMEM((512, 512), BF16),
+            pltpu.VMEM((PER_STEP, 512, 512), BF16),
             pltpu.VMEM((DEVICES, CYCLE, RANK), BF16),
             pltpu.VMEM((32, CYCLE, RANK), BF16),
             pltpu.SemaphoreType.DMA((8,)),

time: 119 us -> 112 us (0.941)
  Pallas kernels: 117 us -> 110 us
    pallas_call x1, Pallas kernels: 85.3 us -> 81.6 us  [local(): pl.pallas_call(exchange_kernel, out_shape=(sds((LEAF_DEV, RANK, RANK), F3...]
    pallas_call x1, Pallas kernels: 11.4 us -> 8.25 us  [local(): pl.pallas_call(pack_kernel, grid=(LEAF_DEV // PER_STEP,), out_shape=(sds(...]
where the time goes in v5:
time: 112 us; the launch traced here: 111 us
  Pallas kernels  110 us (98%)
    pallas_call x1, Pallas kernels, local(): pl.pallas_call(exchange_kernel, out_shape=(sds((LEAF_DEV, RANK, RANK), F3...  81.6 us
    pallas_call x1, Pallas kernels, local(): pl.pallas_call(cholesky_kernel, out_shape=(sds((LEAF_DEV, RANK, RANK), F3...  20.1 us
    pallas_call x1, Pallas kernels, local(): pl.pallas_call(pack_kernel, grid=(LEAF_DEV // PER_STEP,), out_shape=(sds(...  8.25 us

profile of v5, /device:TPU:1, one launch (start us, length us, event | category | flops | bytes accessed | tf_op | source)
XLA Modules:
  0.0 111.4 jit_solution(6932080115041996763)
XLA Ops:
  0.6 0.0 copy-start
  0.6 8.2 %pack.1 = (bf16[256,32,256]{2,1,0:T(8,128)(2,1)}, f32[128,128]{1,0:T(8,128)}) custom-call(bf16[8,512,512]{2,1,0:T(8,128)(2,1)} %dens.1, bf16[512,256]{1,0:T(8,128)(2,1)} %kern.1, s32[16,1024]{1,0:T(8,128)} %bitcast.6, s32[16,1024]{1,0:T(8,128)} %bitcast.7, s32[32,1024]{1,0:T(8,128)} %bitcast.5), custom_call_target="tpu_custom_call" | custom-call | tf_op jit(solution)/shard_map/pack/pallas_call | solution.py:454
  8.9 0.0 copy-done
  8.9 0.0 copy-start.1
  8.9 0.8 copy-done.1
  9.8 81.6 %exchange.1 = (f32[8,256,256]{2,1,0:T(8,128)S(1)}, f32[256,256]{1,0:T(8,128)S(1)}) custom-call(bf16[128,2,32,256]{3,2,1,0:T(8,128)(2,1)} %bitcast.4, f32[128,128]{1,0:T(8,128)S(1)} %copy-done.1, f32[4,256,256]{2,1,0:T(8,128)S(1)} %copy-done), custom_call_target="tpu_custom_call" | custom-call | tf_op jit(solution)/shard_map/exchange/pallas_call | solution.py:483
  91.3 20.1 %cholesky.1 = (f32[8,256,256]{2,1,0:T(8,128)}, f32[1,256,256]{2,1,0:T(8,128)}) custom-call(f32[8,256,256]{2,1,0:T(8,128)S(1)} %get-tuple-element.8.gram, f32[256,256]{1,0:T(8,128)S(1)} %get-tuple-element.9.root), custom_call_target="tpu_custom_call" | custom-call | tf_op jit(solution)/shard_map/cholesky/pallas_call | solution.py:510
Async XLA Ops:
  0.6 8.3 %copy-start = (f32[4,256,256]{2,1,0:T(8,128)S(1)}, f32[4,256,256]{2,1,0:T(8,128)}, u32[]{:S(2)}) copy-start(f32[4,256,256]{2,1,0:T(8,128)} %transfer.1) | copy-start | bytes 3145732
  8.9 0.8 copy-start.1

commit v6 on v5

--- a/solution.py
+++ b/solution.py
@@ -282,7 +282,7 @@
 
     def around(act):
         for shift in range(1, TREE):
-            dc, dz, dy = shift % 2, shift // 2 % 4, shift // 8
+            dc, dz, dy = shift // 16, shift % 4, (shift // 4 + shift) % 4
             place = (my_x * 2 + cs[dc], ys[dy] + zs[dz])
             act(shift, place, cs[dc] * N_SIB + place[1])
 
@@ -330,7 +330,7 @@
         ).wait_recv()
 
     def source_rank(shift):
-        dc, dz, dy = shift % 2, shift // 2 % 4, shift // 8
+        dc, dz, dy = shift // 16, shift % 4, (shift // 4 + shift) % 4
         return cs[dc] * N_SIB + ys[(4 - dy) % 4] + zs[(4 - dz) % 4]
 
     def drain(make):

time: 112 us -> 111 us (level)
  no operation moved by 1% of the time
where the time goes in v6:
time: 111 us
  Pallas kernels  109 us (98%)
    pallas_call x1, Pallas kernels, local(): pl.pallas_call(exchange_kernel, out_shape=(sds((LEAF_DEV, RANK, RANK), F3...  80.9 us
    pallas_call x1, Pallas kernels, local(): pl.pallas_call(cholesky_kernel, out_shape=(sds((LEAF_DEV, RANK, RANK), F3...  20.1 us
    pallas_call x1, Pallas kernels, local(): pl.pallas_call(pack_kernel, grid=(LEAF_DEV // PER_STEP,), out_shape=(sds(...  8.29 us

profile of v6, /device:TPU:1, one launch (start us, length us, event | category | flops | bytes accessed | tf_op | source)
XLA Modules:
  0.0 110.8 jit_solution(4550455814154923374)
XLA Ops:
  0.6 0.0 copy-start
  0.6 8.3 %pack.1 = (bf16[256,32,256]{2,1,0:T(8,128)(2,1)}, f32[128,128]{1,0:T(8,128)}) custom-call(bf16[8,512,512]{2,1,0:T(8,128)(2,1)} %dens.1, bf16[512,256]{1,0:T(8,128)(2,1)} %kern.1, s32[16,1024]{1,0:T(8,128)} %bitcast.6, s32[16,1024]{1,0:T(8,128)} %bitcast.7, s32[32,1024]{1,0:T(8,128)} %bitcast.5), custom_call_target="tpu_custom_call" | custom-call | tf_op jit(solution)/shard_map/pack/pallas_call | solution.py:454
  8.9 0.0 copy-done
  8.9 0.0 copy-start.1
  9.0 0.8 copy-done.1
  9.8 80.9 %exchange.1 = (f32[8,256,256]{2,1,0:T(8,128)S(1)}, f32[256,256]{1,0:T(8,128)S(1)}) custom-call(bf16[128,2,32,256]{3,2,1,0:T(8,128)(2,1)} %bitcast.4, f32[128,128]{1,0:T(8,128)S(1)} %copy-done.1, f32[4,256,256]{2,1,0:T(8,128)S(1)} %copy-done), custom_call_target="tpu_custom_call" | custom-call | tf_op jit(solution)/shard_map/exchange/pallas_call | solution.py:483
  90.7 20.1 %cholesky.1 = (f32[8,256,256]{2,1,0:T(8,128)}, f32[1,256,256]{2,1,0:T(8,128)}) custom-call(f32[8,256,256]{2,1,0:T(8,128)S(1)} %get-tuple-element.8.gram, f32[256,256]{1,0:T(8,128)S(1)} %get-tuple-element.9.root), custom_call_target="tpu_custom_call" | custom-call | tf_op jit(solution)/shard_map/cholesky/pallas_call | solution.py:510
Async XLA Ops:
  0.6 8.3 %copy-start = (f32[4,256,256]{2,1,0:T(8,128)S(1)}, f32[4,256,256]{2,1,0:T(8,128)}, u32[]{:S(2)}) copy-start(f32[4,256,256]{2,1,0:T(8,128)} %transfer.1) | copy-start | bytes 3145732
  8.9 0.8 copy-start.1
